TPU v7x, 32 devices: a whole 2x2x4 slice. The times are simulated.
32 devices in a mesh: ctx: 8 (over y, x, core), shard: 4 (over z).
Axes of the slice: x: 2, y: 2, z: 4, core: 2. Of those that a mesh axis runs over, the one named last changes fastest.
Arguments:
- hidden_in: bfloat16 [8, 4096, 768], P('shard', 'ctx'), may hold values from -6 to 6
- cotangent: bfloat16 [8, 4096, 768], P('shard', 'ctx'), may hold values from -6 to 6
- qkv_weight: bfloat16 [768, 1152], P('shard'), may hold values from -0.21875 to 0.21875
- conv_depth: bfloat16 [9, 768], P(None, 'shard'), may hold values from -2 to 2
- conv_point: bfloat16 [768, 384], P('shard'), may hold values from -0.21875 to 0.21875
- span_weight: bfloat16 [384, 54], P('shard'), may hold values from -0.3125 to 0.3125
- conv_value: bfloat16 [768, 384], P('shard'), may hold values from -0.21875 to 0.21875
- dense_attn: bfloat16 [384, 768], P('shard'), may hold values from -6 to 6
- dense_conv: bfloat16 [384, 768], P('shard'), may hold values from -0.5 to 0.5
- attn_norm_gain: bfloat16 [768], P('shard'), may hold values from 0.5 to 1.5
- attn_norm_bias: bfloat16 [768], P('shard'), may hold values from -1.25 to 1.25
- ffn_inner: bfloat16 [2, 384, 1536], P(None, 'shard'), may hold values from -0.3125 to 0.3125
- ffn_outer: bfloat16 [2, 1536, 384], P(None, 'shard'), may hold values from -0.15625 to 0.15625
- out_norm_gain: bfloat16 [768], P('shard'), may hold values from 0.5 to 1.5
- out_norm_bias: bfloat16 [768], P('shard'), may hold values from -1.25 to 1.25
Outputs:
- layer_out: bfloat16 [8, 4096, 768], P('shard', 'ctx')
- grad_in: float32 [8, 4096, 768], P('shard', 'ctx')
- grad_qkv: float32 [768, 1152], P('shard')
- grad_depth: float32 [9, 768], P(None, 'shard')
- grad_point: float32 [768, 384], P('shard')
- grad_span: float32 [384, 54], P('shard')
- grad_conv_value: float32 [768, 384], P('shard')
- grad_dense_attn: float32 [384, 768], P('shard')
- grad_dense_conv: float32 [384, 768], P('shard')
- grad_attn_gain: float32 [768], P('shard')
- grad_attn_bias: float32 [768], P('shard')
- grad_ffn_inner: float32 [2, 384, 1536], P(None, 'shard')
- grad_ffn_outer: float32 [2, 1536, 384], P(None, 'shard')
- grad_out_gain: float32 [768], P('shard')
- grad_out_bias: float32 [768], P('shard')
All inputs are finite; a program needn't handle non-finite values.
Results may differ from a plain program's by a relative error of at most 0.025.
Values may be sent and summed in bfloat16 or wider, within the bound.
A program may use at most 192 MiB of HBM per device.

v0:
```python
from functools import partial
import math

import jax
import jax.numpy as jnp
from jax import lax
from jax.sharding import PartitionSpec as P

D = 768
HEADS = 6
HEAD = 64
GROUPS = 2
KERNEL = 9


norm_eps = 1e-12


def with_halo(block, sides, width):
    for axis, dim in sides:
        count = lax.axis_size(axis)
        forward = [(i, i + 1) for i in range(count - 1)]
        backward = [(target, source) for source, target in forward]
        low = lax.ppermute(
            lax.slice_in_dim(block, block.shape[dim] - width, None, axis=dim), axis, forward
        )
        high = lax.ppermute(lax.slice_in_dim(block, 0, width, axis=dim), axis, backward)
        block = jnp.concatenate([low, block, high], axis=dim)
    return block


def shifted(value, axis, by):
    devices = lax.axis_size(axis)
    return lax.ppermute(value, axis, [(i, (i + by) % devices) for i in range(devices)])


def layer_norm(hidden, norm_gain, norm_bias):
    center = hidden - jnp.mean(hidden, axis=-1, keepdims=True)
    inv_std = lax.rsqrt(jnp.mean(center * center, axis=-1, keepdims=True) + norm_eps)
    normed = center * inv_std
    return (normed * norm_gain + norm_bias, normed, inv_std)


def norm_back(normed, inv_std, norm_gain, d_result):
    d_gain = jnp.sum(d_result * normed, axis=(0, 1))
    d_shift = jnp.sum(d_result, axis=(0, 1))
    d_scaled = d_result * norm_gain
    d_hidden = inv_std * (
        d_scaled
        - jnp.mean(d_scaled, axis=-1, keepdims=True)
        - normed * jnp.mean(d_scaled * normed, axis=-1, keepdims=True)
    )
    return (d_hidden, d_gain, d_shift)


def four_heads(values):
    return values.reshape(values.shape[0], values.shape[1], HEADS, HEAD)


def attend_fold(query_four, running, shard_piece):
    attn_width = HEADS * HEAD
    piece_rows = shard_piece.shape[1]
    step_rows = math.gcd(piece_rows, 256)
    score_scale = 1.0 / math.sqrt(HEAD)

    def key_step(step_index, current):
        row_top, row_total, weighted = current
        key_block = lax.dynamic_slice_in_dim(shard_piece, step_index * step_rows, step_rows, 1)
        keys_four = four_heads(key_block[..., :attn_width])
        values_four = four_heads(key_block[..., attn_width:])
        scores = (
            jnp.einsum("sqhe,skhe->sqhk", query_four, keys_four, preferred_element_type=jnp.float32)
            * score_scale
        )
        new_top = jnp.maximum(row_top, jnp.max(scores, axis=-1))
        exp_scores = jnp.exp(scores - new_top[..., None])
        rescale = jnp.exp(row_top - new_top)
        row_total = row_total * rescale + jnp.sum(exp_scores, axis=-1)
        weighted = weighted * rescale[..., None] + jnp.einsum(
            "sqhk,skhe->sqhe",
            exp_scores.astype(jnp.bfloat16),
            values_four,
            preferred_element_type=jnp.float32,
        )
        return (new_top, row_total, weighted)

    return lax.fori_loop(0, piece_rows // step_rows, key_step, running)


def attend_back(query_four, grad_four, row_lse, row_delta, keys_four, values_four):
    score_scale = 1.0 / math.sqrt(HEAD)
    scores = (
        jnp.einsum("sqhe,skhe->sqhk", query_four, keys_four, preferred_element_type=jnp.float32)
        * score_scale
    )
    attend_probs = jnp.exp(scores - row_lse[..., None])
    d_probs = jnp.einsum(
        "sqhe,skhe->sqhk", grad_four, values_four, preferred_element_type=jnp.float32
    )
    d_scores = (attend_probs * (d_probs - row_delta[..., None])).astype(jnp.bfloat16)
    d_query = (
        jnp.einsum("sqhk,skhe->sqhe", d_scores, keys_four, preferred_element_type=jnp.float32)
        * score_scale
    )
    d_key = (
        jnp.einsum("sqhk,sqhe->skhe", d_scores, query_four, preferred_element_type=jnp.float32)
        * score_scale
    )
    d_value = jnp.einsum(
        "sqhk,sqhe->skhe",
        attend_probs.astype(jnp.bfloat16),
        grad_four,
        preferred_element_type=jnp.float32,
    )
    return (d_query, d_key, d_value)


def shards(
    hidden_in,
    cotangent,
    qkv_weight,
    conv_depth,
    conv_point,
    span_weight,
    conv_value,
    dense_attn,
    dense_conv,
    attn_norm_gain,
    attn_norm_bias,
    ffn_inner,
    ffn_outer,
    out_norm_gain,
    out_norm_bias,
):
    attn_width = HEADS * HEAD
    half_kernel = KERNEL // 2
    seq_count, local_rows, model_width = hidden_in.shape
    gathered = (
        lax.all_gather(qkv_weight, "shard", axis=0, tiled=True),
        lax.all_gather(conv_depth, "shard", axis=1, tiled=True),
        lax.all_gather(conv_point, "shard", axis=0, tiled=True),
        lax.all_gather(span_weight, "shard", axis=0, tiled=True),
        lax.all_gather(conv_value, "shard", axis=0, tiled=True),
        lax.all_gather(dense_attn, "shard", axis=0, tiled=True),
        lax.all_gather(dense_conv, "shard", axis=0, tiled=True),
        lax.all_gather(attn_norm_gain, "shard", axis=0, tiled=True),
        lax.all_gather(attn_norm_bias, "shard", axis=0, tiled=True),
        lax.all_gather(ffn_inner, "shard", axis=1, tiled=True),
        lax.all_gather(ffn_outer, "shard", axis=1, tiled=True),
        lax.all_gather(out_norm_gain, "shard", axis=0, tiled=True),
        lax.all_gather(out_norm_bias, "shard", axis=0, tiled=True),
    )
    (
        full_qkv,
        full_depth,
        full_point,
        full_span,
        full_value,
        full_dense_attn,
        full_dense_conv,
        attn_gain_full,
        attn_bias_full,
        full_inner,
        full_outer,
        out_gain_full,
        out_bias_full,
    ) = gathered
    rows_ext = with_halo(hidden_in, (("ctx", 1),), half_kernel)
    mixed_qkv = jnp.einsum("sti,io->sto", hidden_in, full_qkv, preferred_element_type=jnp.float32)
    query_low = mixed_qkv[..., :attn_width].astype(jnp.bfloat16)
    pair_low = mixed_qkv[..., attn_width:].astype(jnp.bfloat16)
    query_four = four_heads(query_low)
    start_state = (
        jnp.full((seq_count, local_rows, HEADS), -jnp.inf, jnp.float32),
        jnp.zeros((seq_count, local_rows, HEADS), jnp.float32),
        jnp.zeros((seq_count, local_rows, HEADS, HEAD), jnp.float32),
    )
    row_top, row_total, weighted = attend_fold(
        query_four, start_state, lax.all_gather(pair_low, "ctx", axis=1, tiled=True)
    )
    row_lse = row_top + jnp.log(row_total)
    context = weighted / row_total[..., None]
    context_low = context.reshape(seq_count, local_rows, attn_width).astype(jnp.bfloat16)
    depth_fwd = full_depth.astype(jnp.float32)
    spread = rows_ext[:, 0:local_rows].astype(jnp.float32) * depth_fwd[0]
    for offset in range(1, KERNEL):
        spread = (
            spread
            + rows_ext[:, offset : offset + local_rows].astype(jnp.float32) * depth_fwd[offset]
        )
    spread_low = spread.astype(jnp.bfloat16)
    key_conv = jnp.einsum("sti,ia->sta", spread_low, full_point, preferred_element_type=jnp.float32)
    query_f32 = query_low.astype(jnp.float32)
    span_mix = (key_conv * query_f32).astype(jnp.bfloat16)
    logits = jnp.einsum("sta,ak->stk", span_mix, full_span, preferred_element_type=jnp.float32)
    logits = logits.reshape(seq_count, local_rows, HEADS, KERNEL)
    logit_top = jnp.max(logits, axis=-1, keepdims=True)
    exp_logits = jnp.exp(logits - logit_top)
    kernel_soft = exp_logits / jnp.sum(exp_logits, axis=-1, keepdims=True)
    value_ext = jnp.einsum("sti,ia->sta", rows_ext, full_value, preferred_element_type=jnp.float32)
    value_ext = four_heads(value_ext)
    conv_res = kernel_soft[..., 0:1] * value_ext[:, 0:local_rows]
    for offset in range(1, KERNEL):
        conv_res = (
            conv_res
            + kernel_soft[..., offset : offset + 1] * value_ext[:, offset : offset + local_rows]
        )
    conv_low = conv_res.reshape(seq_count, local_rows, attn_width).astype(jnp.bfloat16)
    dense_sum = jnp.einsum(
        "sta,ai->sti", context_low, full_dense_attn, preferred_element_type=jnp.float32
    ) + jnp.einsum("sta,ai->sti", conv_low, full_dense_conv, preferred_element_type=jnp.float32)
    hidden_one, normed_one, inv_one = layer_norm(
        dense_sum + hidden_in.astype(jnp.float32),
        attn_gain_full.astype(jnp.float32),
        attn_bias_full.astype(jnp.float32),
    )
    hidden_low = hidden_one.astype(jnp.bfloat16).reshape(seq_count, local_rows, GROUPS, D // GROUPS)
    inner_act = jnp.einsum(
        "stgi,gio->stgo", hidden_low, full_inner, preferred_element_type=jnp.float32
    )
    active, gelu_pull = jax.vjp(partial(jax.nn.gelu, approximate=False), inner_act)
    active_low = active.astype(jnp.bfloat16)
    outer_sum = jnp.einsum(
        "stgo,goi->stgi", active_low, full_outer, preferred_element_type=jnp.float32
    )
    outer_sum = outer_sum.reshape(seq_count, local_rows, model_width)
    layer_f32, normed_two, inv_two = layer_norm(
        outer_sum + hidden_one, out_gain_full.astype(jnp.float32), out_bias_full.astype(jnp.float32)
    )
    layer_out = layer_f32.astype(jnp.bfloat16)
    d_second, grad_out_gain, grad_out_bias = norm_back(
        normed_two, inv_two, out_gain_full.astype(jnp.float32), cotangent.astype(jnp.float32)
    )
    d_outer_low = d_second.astype(jnp.bfloat16).reshape(seq_count, local_rows, GROUPS, D // GROUPS)
    grad_ffn_outer = jnp.einsum(
        "stgo,stgi->goi", active_low, d_outer_low, preferred_element_type=jnp.float32
    )
    d_active = jnp.einsum(
        "stgi,goi->stgo", d_outer_low, full_outer, preferred_element_type=jnp.float32
    )
    d_inner_low = gelu_pull(d_active)[0].astype(jnp.bfloat16)
    grad_ffn_inner = jnp.einsum(
        "stgi,stgo->gio", hidden_low, d_inner_low, preferred_element_type=jnp.float32
    )
    d_hidden = jnp.einsum(
        "stgo,gio->stgi", d_inner_low, full_inner, preferred_element_type=jnp.float32
    )
    d_hidden = d_hidden.reshape(seq_count, local_rows, model_width) + d_second
    d_first, grad_attn_gain, grad_attn_bias = norm_back(
        normed_one, inv_one, attn_gain_full.astype(jnp.float32), d_hidden
    )
    d_dense_low = d_first.astype(jnp.bfloat16)
    grad_dense_attn = jnp.einsum(
        "sta,sti->ai", context_low, d_dense_low, preferred_element_type=jnp.float32
    )
    grad_dense_conv = jnp.einsum(
        "sta,sti->ai", conv_low, d_dense_low, preferred_element_type=jnp.float32
    )
    d_context_low = jnp.einsum(
        "sti,ai->sta", d_dense_low, full_dense_attn, preferred_element_type=jnp.float32
    ).astype(jnp.bfloat16)
    d_conv_res = four_heads(
        jnp.einsum("sti,ai->sta", d_dense_low, full_dense_conv, preferred_element_type=jnp.float32)
    )
    d_kernel = jnp.concatenate(
        [
            jnp.sum(d_conv_res * value_ext[:, offset : offset + local_rows], axis=-1, keepdims=True)
            for offset in range(KERNEL)
        ],
        axis=-1,
    )
    d_logits = kernel_soft * (d_kernel - jnp.sum(d_kernel * kernel_soft, axis=-1, keepdims=True))
    d_logits_low = d_logits.reshape(seq_count, local_rows, HEADS * KERNEL).astype(jnp.bfloat16)
    grad_span = jnp.einsum(
        "sta,stk->ak", span_mix, d_logits_low, preferred_element_type=jnp.float32
    )
    d_mix = jnp.einsum("stk,ak->sta", d_logits_low, full_span, preferred_element_type=jnp.float32)
    d_key_low = (d_mix * query_f32).astype(jnp.bfloat16)
    d_query_conv = d_mix * key_conv
    grad_point = jnp.einsum(
        "sti,sta->ia", spread_low, d_key_low, preferred_element_type=jnp.float32
    )
    d_spread = jnp.einsum("sta,ia->sti", d_key_low, full_point, preferred_element_type=jnp.float32)
    grad_depth = jnp.stack(
        [
            jnp.sum(
                d_spread * rows_ext[:, offset : offset + local_rows].astype(jnp.float32),
                axis=(0, 1),
            )
            for offset in range(KERNEL)
        ],
        axis=0,
    )
    ext_rows = local_rows + 2 * half_kernel
    d_rows_ext = jnp.zeros((seq_count, ext_rows, model_width), jnp.float32)
    d_value_ext = jnp.zeros((seq_count, ext_rows, HEADS, HEAD), jnp.float32)
    for offset in range(KERNEL):
        d_rows_ext = d_rows_ext + jnp.pad(
            d_spread * depth_fwd[offset], ((0, 0), (offset, 2 * half_kernel - offset), (0, 0))
        )
        d_value_ext = d_value_ext + jnp.pad(
            kernel_soft[..., offset : offset + 1] * d_conv_res,
            ((0, 0), (offset, 2 * half_kernel - offset), (0, 0), (0, 0)),
        )
    grad_ext = jnp.concatenate(
        [d_value_ext.reshape(seq_count, ext_rows, attn_width), d_rows_ext], axis=-1
    )
    edge_rims = jnp.concatenate(
        [grad_ext[:, :half_kernel], grad_ext[:, ext_rows - half_kernel :]], axis=1
    )
    edge_sums = with_halo(edge_rims.astype(jnp.bfloat16), (("ctx", 1),), half_kernel).astype(
        edge_rims.dtype
    )
    own_rows = grad_ext[:, half_kernel : half_kernel + local_rows]
    own_rows = jnp.concatenate(
        [
            own_rows[:, :half_kernel] + edge_sums[:, :half_kernel],
            own_rows[:, half_kernel : local_rows - half_kernel],
            own_rows[:, local_rows - half_kernel :] + edge_sums[:, 3 * half_kernel :],
        ],
        axis=1,
    )
    d_value_low = own_rows[..., :attn_width].astype(jnp.bfloat16)
    d_rows_conv = own_rows[..., attn_width:]
    grad_conv_value = jnp.einsum(
        "sti,sta->ia", hidden_in, d_value_low, preferred_element_type=jnp.float32
    )
    grad_four = four_heads(d_context_low)
    row_delta = jnp.sum(grad_four.astype(jnp.float32) * context, axis=-1)

    def keys_turn(step_index, current):
        packet, grad_pack, query_sum = current
        d_query, d_key, d_value = attend_back(
            query_four,
            grad_four,
            row_lse,
            row_delta,
            four_heads(packet[..., :attn_width]),
            four_heads(packet[..., attn_width:]),
        )
        grad_pack = grad_pack + jnp.concatenate(
            [
                d_key.reshape(seq_count, local_rows, attn_width),
                d_value.reshape(seq_count, local_rows, attn_width),
            ],
            axis=-1,
        )
        packet = shifted(packet, "ctx", 1)
        grad_pack = shifted(grad_pack.astype(jnp.bfloat16), "ctx", 1).astype(grad_pack.dtype)
        return (packet, grad_pack, query_sum + d_query)

    finished = lax.fori_loop(
        0,
        lax.axis_size("ctx"),
        keys_turn,
        (
            pair_low,
            jnp.zeros((seq_count, local_rows, 2 * attn_width), jnp.float32),
            jnp.zeros((seq_count, local_rows, HEADS, HEAD), jnp.float32),
        ),
    )
    d_query_attn = finished[2].reshape(seq_count, local_rows, attn_width)
    d_pair = finished[1]
    d_query_low = (d_query_attn + d_query_conv).astype(jnp.bfloat16)
    d_all_low = jnp.concatenate([d_query_low, d_pair.astype(jnp.bfloat16)], axis=-1)
    grad_qkv = jnp.einsum("sti,sto->io", hidden_in, d_all_low, preferred_element_type=jnp.float32)
    grad_in = (
        d_first
        + jnp.einsum("sto,io->sti", d_all_low, full_qkv, preferred_element_type=jnp.float32)
        + jnp.einsum("sta,ia->sti", d_value_low, full_value, preferred_element_type=jnp.float32)
        + d_rows_conv
    )
    shared = (
        lax.psum_scatter(
            grad_qkv.astype(jnp.bfloat16), "shard", scatter_dimension=0, tiled=True
        ).astype(jnp.float32),
        lax.psum_scatter(
            grad_depth.astype(jnp.bfloat16), "shard", scatter_dimension=1, tiled=True
        ).astype(jnp.float32),
        lax.psum_scatter(
            grad_point.astype(jnp.bfloat16), "shard", scatter_dimension=0, tiled=True
        ).astype(jnp.float32),
        lax.psum_scatter(
            grad_span.astype(jnp.bfloat16), "shard", scatter_dimension=0, tiled=True
        ).astype(jnp.float32),
        lax.psum_scatter(
            grad_conv_value.astype(jnp.bfloat16), "shard", scatter_dimension=0, tiled=True
        ).astype(jnp.float32),
        lax.psum_scatter(
            grad_dense_attn.astype(jnp.bfloat16), "shard", scatter_dimension=0, tiled=True
        ).astype(jnp.float32),
        lax.psum_scatter(
            grad_dense_conv.astype(jnp.bfloat16), "shard", scatter_dimension=0, tiled=True
        ).astype(jnp.float32),
        lax.psum_scatter(
            grad_attn_gain.astype(jnp.bfloat16), "shard", scatter_dimension=0, tiled=True
        ).astype(jnp.float32),
        lax.psum_scatter(
            grad_attn_bias.astype(jnp.bfloat16), "shard", scatter_dimension=0, tiled=True
        ).astype(jnp.float32),
        lax.psum_scatter(
            grad_ffn_inner.astype(jnp.bfloat16), "shard", scatter_dimension=1, tiled=True
        ).astype(jnp.float32),
        lax.psum_scatter(
            grad_ffn_outer.astype(jnp.bfloat16), "shard", scatter_dimension=1, tiled=True
        ).astype(jnp.float32),
        lax.psum_scatter(
            grad_out_gain.astype(jnp.bfloat16), "shard", scatter_dimension=0, tiled=True
        ).astype(jnp.float32),
        lax.psum_scatter(
            grad_out_bias.astype(jnp.bfloat16), "shard", scatter_dimension=0, tiled=True
        ).astype(jnp.float32),
    )
    summed = (
        lax.psum(shared[0].astype(jnp.bfloat16), "ctx").astype(jnp.float32),
        lax.psum(shared[1].astype(jnp.bfloat16), "ctx").astype(jnp.float32),
        lax.psum(shared[2].astype(jnp.bfloat16), "ctx").astype(jnp.float32),
        lax.psum(shared[3].astype(jnp.bfloat16), "ctx").astype(jnp.float32),
        lax.psum(shared[4].astype(jnp.bfloat16), "ctx").astype(jnp.float32),
        lax.psum(shared[5].astype(jnp.bfloat16), "ctx").astype(jnp.float32),
        lax.psum(shared[6].astype(jnp.bfloat16), "ctx").astype(jnp.float32),
        lax.psum(shared[7].astype(jnp.bfloat16), "ctx").astype(jnp.float32),
        lax.psum(shared[8].astype(jnp.bfloat16), "ctx").astype(jnp.float32),
        lax.psum(shared[9].astype(jnp.bfloat16), "ctx").astype(jnp.float32),
        lax.psum(shared[10].astype(jnp.bfloat16), "ctx").astype(jnp.float32),
        lax.psum(shared[11].astype(jnp.bfloat16), "ctx").astype(jnp.float32),
        lax.psum(shared[12].astype(jnp.bfloat16), "ctx").astype(jnp.float32),
    )
    result_grads = tuple(summed)
    return (layer_out, grad_in) + result_grads


def solution(mesh):
    return jax.shard_map(
        shards,
        mesh=mesh,
        in_specs=(
            P("shard", "ctx", None),
            P("shard", "ctx", None),
            P("shard", None),
            P(None, "shard"),
            P("shard", None),
            P("shard", None),
            P("shard", None),
            P("shard", None),
            P("shard", None),
            P("shard"),
            P("shard"),
            P(None, "shard", None),
            P(None, "shard", None),
            P("shard"),
            P("shard"),
        ),
        out_specs=(
            P("shard", "ctx", None),
            P("shard", "ctx", None),
            P("shard", None),
            P(None, "shard"),
            P("shard", None),
            P("shard", None),
            P("shard", None),
            P("shard", None),
            P("shard", None),
            P("shard"),
            P("shard"),
            P(None, "shard", None),
            P(None, "shard", None),
            P("shard"),
            P("shard"),
        ),
        check_vma=False,
    )
```

profile of v0, /device:TPU:0, one launch (start us, length us, event | category | flops | bytes accessed | tf_op | source)
XLA Modules:
  0.0 1392.4 jit_solution(8333126669531813735)
XLA Ops:
  8.0 44.7 %all-gather.7.cloned.1.call-done = bf16[768,1152]{1,0:T(8,128)(2,1)} async-done(((bf16[192,1152]{1,0:T(8,128)(2,1)}), bf16[768,1152]{1,0:T(8,128)(2,1)}) %all-gather.7.cloned.1.call-update) | async-done | bytes 1769488 | tf_op jit(solution)/shard_map/all_gather | solution.py:139
  69.4 9.9 all-reduce.29
  79.9 13.1 all-gather
  93.3 15.6 %all_gather.46 = bf16[768,384]{1,0:T(8,128)(2,1)S(1)} all-gather(bf16[192,384]{1,0:T(8,128)(2,1)S(1)} %copy-done.67), channel_id=1, replica_groups=mesh['ctx'=8,'shard'=4] {'shard'}, dimensions={0}, use_global_device_ids=true | all-gather | bytes 737280 | tf_op jit(solution)/shard_map/all_gather | solution.py:141
  108.9 16.1 %all_gather.48 = bf16[768,384]{1,0:T(8,128)(2,1)S(1)} all-gather(bf16[192,384]{1,0:T(8,128)(2,1)S(1)} %copy-done.68), channel_id=1, replica_groups=mesh['ctx'=8,'shard'=4] {'shard'}, dimensions={0}, use_global_device_ids=true | all-gather | bytes 737280 | tf_op jit(solution)/shard_map/all_gather | solution.py:143
  125.1 17.0 %all_gather.44 = bf16[384,768]{1,0:T(8,128)(2,1)} all-gather(bf16[96,768]{1,0:T(8,128)(2,1)S(1)} %copy-done.69), channel_id=1, replica_groups=mesh['ctx'=8,'shard'=4] {'shard'}, dimensions={0}, use_global_device_ids=true | all-gather | bytes 737280 | tf_op jit(solution)/shard_map/all_gather | solution.py:144
  142.1 20.9 %all_gather.49 = bf16[384,768]{1,0:T(8,128)(2,1)} all-gather(bf16[96,768]{1,0:T(8,128)(2,1)S(1)} %copy-done.70), channel_id=1, replica_groups=mesh['ctx'=8,'shard'=4] {'shard'}, dimensions={0}, use_global_device_ids=true | all-gather | bytes 737280 | tf_op jit(solution)/shard_map/all_gather | solution.py:145
  163.0 14.1 %all-gather.1 = bf16[4,96,54]{1,2,0:T(8,128)(2,1)S(1)} all-gather(bf16[1,96,54]{1,2,0:T(8,128)(2,1)S(1)} %bitcast.405), channel_id=1, replica_groups=mesh['ctx'=8,'shard'=4] {'shard'}, dimensions={0}, use_global_device_ids=true | all-gather | bytes 51840 | tf_op jit(solution)/shard_map/all_gather | solution.py:142
  210.5 105.8 %while.33 = (s32[]{:T(128)}, f32[2,512,6]{1,2,0:T(8,128)S(1)}, f32[2,512,6]{1,2,0:T(8,128)S(1)}, f32[2,512,6,64]{1,3,2,0:T(8,128)}, bf16[2,4096,768]{2,1,0:T(8,1...) while((s32[]{:T(128)}, f32[2,512,6]{1,2,0:T(8,128)S(1)}, ...), condition=%wide.region_3.0_spmd.clone, body=%wide.region_0.0_spmd.clone.sunk | while | flops 416446464 | bytes 39715064 | solution.py:87
  332.1 33.1 %fusion.30 = (bf16[2,512,2,1536]{3,1,0,2:T(8,128)(2,1)}, f32[2,512,2,1536]{3,1,0,2:T(8,128)}, f32[2,2,512,1536]{3,2,1,0:T(8,128)}) fusion(bf16[2,512,2,384]{1,3,0,2:T(8,128)(2,1)} %copy.197, bf16[2,384,1536]{2,1,0:T(8,128)(2,1)} %all-gather.11.cloned.1.call-done), kind=kOutput, calls=%fused_computation.48 | convolution fusion | flops 2620391424 | bytes 35389440 | tf_op jit(solution)/shard_map/stgi,gio->stgo/dot_general | solution.py:218
  394.5 13.2 fusion.27
  445.3 530.1 %while.34 = (s32[]{:T(128)}, bf16[2,512,768]{1,2,0:T(8,128)(2,1)}, f32[2,512,768]{1,2,0:T(8,128)}, f32[2,512,6,64]{1,3,2,0:T(8,128)}, bf16[2,512,6,64]{1,3,2,0:T...) while((s32[]{:T(128)}, bf16[2,512,768]{1,2,0:T(8,128)(2,1)}, ...), condition=%wide.region_16.0_spmd.clone, body=%wide.region_15.0_spmd.clone.sunk | while | flops 2043936768 | bytes 99950776 | solution.py:352
  455.9 7.8 fusion.233
  483.4 10.6 collective-permute-done.1
  496.1 14.8 %collective-permute-done = bf16[2,512,768]{1,2,0:T(8,128)(2,1)} collective-permute-done((bf16[2,512,768]{1,2,0:T(8,128)(2,1)}, bf16[2,512,768]{1,2,0:T(8,128)(2,1)}, u32[]{:S(2)}, u32[]{:S(2)}) %collective-permute-start) | collective-permute-done | bytes 1572896 | tf_op jit(solution)/shard_map/while/body/eval_jaxpr/ppermute | solution.py:34
  521.3 7.8 fusion.233
  549.2 11.0 collective-permute-done.1
  562.4 14.8 %collective-permute-done = bf16[2,512,768]{1,2,0:T(8,128)(2,1)} collective-permute-done((bf16[2,512,768]{1,2,0:T(8,128)(2,1)}, bf16[2,512,768]{1,2,0:T(8,128)(2,1)}, u32[]{:S(2)}, u32[]{:S(2)}) %collective-permute-start) | collective-permute-done | bytes 1572896 | tf_op jit(solution)/shard_map/while/body/eval_jaxpr/ppermute | solution.py:34
  587.6 7.8 fusion.233
  614.7 11.9 collective-permute-done.1
  628.8 14.8 %collective-permute-done = bf16[2,512,768]{1,2,0:T(8,128)(2,1)} collective-permute-done((bf16[2,512,768]{1,2,0:T(8,128)(2,1)}, bf16[2,512,768]{1,2,0:T(8,128)(2,1)}, u32[]{:S(2)}, u32[]{:S(2)}) %collective-permute-start) | collective-permute-done | bytes 1572896 | tf_op jit(solution)/shard_map/while/body/eval_jaxpr/ppermute | solution.py:34
  653.9 7.8 fusion.233
  680.1 12.8 collective-permute-done.1
  695.1 14.8 %collective-permute-done = bf16[2,512,768]{1,2,0:T(8,128)(2,1)} collective-permute-done((bf16[2,512,768]{1,2,0:T(8,128)(2,1)}, bf16[2,512,768]{1,2,0:T(8,128)(2,1)}, u32[]{:S(2)}, u32[]{:S(2)}) %collective-permute-start) | collective-permute-done | bytes 1572896 | tf_op jit(solution)/shard_map/while/body/eval_jaxpr/ppermute | solution.py:34
  720.3 7.8 fusion.233
  745.6 13.7 collective-permute-done.1
  761.4 14.8 %collective-permute-done = bf16[2,512,768]{1,2,0:T(8,128)(2,1)} collective-permute-done((bf16[2,512,768]{1,2,0:T(8,128)(2,1)}, bf16[2,512,768]{1,2,0:T(8,128)(2,1)}, u32[]{:S(2)}, u32[]{:S(2)}) %collective-permute-start) | collective-permute-done | bytes 1572896 | tf_op jit(solution)/shard_map/while/body/eval_jaxpr/ppermute | solution.py:34
  786.6 7.8 fusion.233
  811.0 14.6 %collective-permute-done.1 = bf16[2,512,768]{1,2,0:T(8,128)(2,1)S(1)} collective-permute-done((bf16[2,512,768]{1,2,0:T(8,128)(2,1)}, bf16[2,512,768]{1,2,0:T(8,128)(2,1)S(1)}, u32[]{:S(2)}, u32[]{:S(2)}) %collective-permute-start.1) | collective-permute-done | bytes 1572896 | tf_op jit(solution)/shard_map/while/body/eval_jaxpr/ppermute | solution.py:34
  827.8 14.8 %collective-permute-done = bf16[2,512,768]{1,2,0:T(8,128)(2,1)} collective-permute-done((bf16[2,512,768]{1,2,0:T(8,128)(2,1)}, bf16[2,512,768]{1,2,0:T(8,128)(2,1)}, u32[]{:S(2)}, u32[]{:S(2)}) %collective-permute-start) | collective-permute-done | bytes 1572896 | tf_op jit(solution)/shard_map/while/body/eval_jaxpr/ppermute | solution.py:34
  853.0 7.8 fusion.233
  876.6 15.4 %collective-permute-done.1 = bf16[2,512,768]{1,2,0:T(8,128)(2,1)S(1)} collective-permute-done((bf16[2,512,768]{1,2,0:T(8,128)(2,1)}, bf16[2,512,768]{1,2,0:T(8,128)(2,1)S(1)}, u32[]{:S(2)}, u32[]{:S(2)}) %collective-permute-start.1) | collective-permute-done | bytes 1572896 | tf_op jit(solution)/shard_map/while/body/eval_jaxpr/ppermute | solution.py:34
  894.1 14.8 %collective-permute-done = bf16[2,512,768]{1,2,0:T(8,128)(2,1)} collective-permute-done((bf16[2,512,768]{1,2,0:T(8,128)(2,1)}, bf16[2,512,768]{1,2,0:T(8,128)(2,1)}, u32[]{:S(2)}, u32[]{:S(2)}) %collective-permute-start) | collective-permute-done | bytes 1572896 | tf_op jit(solution)/shard_map/while/body/eval_jaxpr/ppermute | solution.py:34
  919.3 7.8 fusion.233
  942.9 15.4 %collective-permute-done.1 = bf16[2,512,768]{1,2,0:T(8,128)(2,1)S(1)} collective-permute-done((bf16[2,512,768]{1,2,0:T(8,128)(2,1)}, bf16[2,512,768]{1,2,0:T(8,128)(2,1)S(1)}, u32[]{:S(2)}, u32[]{:S(2)}) %collective-permute-start.1) | collective-permute-done | bytes 1572896 | tf_op jit(solution)/shard_map/while/body/eval_jaxpr/ppermute | solution.py:34
  960.5 14.8 %collective-permute-done = bf16[2,512,768]{1,2,0:T(8,128)(2,1)} collective-permute-done((bf16[2,512,768]{1,2,0:T(8,128)(2,1)}, bf16[2,512,768]{1,2,0:T(8,128)(2,1)}, u32[]{:S(2)}, u32[]{:S(2)}) %collective-permute-start) | collective-permute-done | bytes 1572896 | tf_op jit(solution)/shard_map/while/body/eval_jaxpr/ppermute | solution.py:34
  979.4 10.5 pad_add_fusion.1
  992.9 12.9 fusion.65
  1045.9 8.3 bitcast_convert_fusion
  1068.0 26.9 %reduce-scatter.28.cloned.1.call-done = bf16[192,1152]{1,0:T(8,128)(2,1)} async-done(((bf16[768,1152]{1,0:T(8,128)(2,1)}), bf16[192,1152]{1,0:T(8,128)(2,1)}) %reduce-scatter.28.cloned.1.call-update) | async-done | bytes 442384
  1097.0 21.5 %reduce-scatter.20.cloned.1.call-done = bf16[96,768]{1,0:T(8,128)(2,1)} async-done(((bf16[384,768]{1,0:T(8,128)(2,1)}), bf16[96,768]{1,0:T(8,128)(2,1)}) %reduce-scatter.20.cloned.1.call-update) | async-done | bytes 147472 | tf_op jit(solution)/shard_map/reduce_scatter | solution.py:389
  1118.4 22.6 %reduce-scatter.22.cloned.1.call-done = bf16[96,768]{1,0:T(8,128)(2,1)} async-done(((bf16[384,768]{1,0:T(8,128)(2,1)}), bf16[96,768]{1,0:T(8,128)(2,1)}) %reduce-scatter.22.cloned.1.call-update) | async-done | bytes 147472 | tf_op jit(solution)/shard_map/reduce_scatter | solution.py:392
  1141.1 23.4 %reduce-scatter.18.cloned.1.call-done = bf16[192,384]{1,0:T(8,128)(2,1)} async-done(((bf16[768,384]{1,0:T(8,128)(2,1)}), bf16[192,384]{1,0:T(8,128)(2,1)}) %reduce-scatter.18.cloned.1.call-update) | async-done | bytes 147472 | tf_op jit(solution)/shard_map/reduce_scatter | solution.py:380
  1164.4 48.7 %reduce-scatter.26.cloned.1.call-done = bf16[2,384,384]{2,1,0:T(8,128)(2,1)} async-done(((bf16[2,1536,384]{2,1,0:T(8,128)(2,1)}), bf16[2,384,384]{2,1,0:T(8,128)(2,1)}) %reduce-scatter.26.cloned.1.call-update) | async-done | bytes 589840 | tf_op jit(solution)/shard_map/reduce_scatter | solution.py:404
  1213.1 50.0 %reduce-scatter.24.cloned.1.call-done = bf16[2,96,1536]{2,1,0:T(8,128)(2,1)} async-done(((bf16[2,384,1536]{2,1,0:T(8,128)(2,1)}), bf16[2,96,1536]{2,1,0:T(8,128)(2,1)}) %reduce-scatter.24.cloned.1.call-update) | async-done | bytes 589840 | tf_op jit(solution)/shard_map/reduce_scatter | solution.py:401
  1269.1 17.1 %all-reduce.28 = (bf16[768]{0:T(1024)(128)(2,1)S(1)}, bf16[768]{0:T(1024)(128)(2,1)S(1)}, bf16[768]{0:T(1024)(128)(2,1)S(1)}, bf16[768]{0:T(1024)(128)(2,1)S(1)}, bf16[768]{0:T(1024)(128)(2,1)S(1)}) all-reduce(bf16[768]{0:T(1024)(128)(2,1)S(1)} %dynamic-update-slice.3, ...), channel_id=1, replica_groups=mesh['ctx'=8,'shard'=4] {'shard'}, use_global_device_ids=true, to_apply=%add.21 | all-reduce | flops 3840 | bytes 15360
  1305.8 22.8 %all-reduce.26 = (bf16[9,192]{1,0:T(8,128)(2,1)S(1)}, bf16[96,54]{0,1:T(8,128)(2,1)S(1)}, bf16[192]{0:T(256)(128)(2,1)S(1)}, bf16[192]{0:T(256)(128)(2,1)S(1)}, ...) all-reduce(bf16[9,192]{1,0:T(8,128)(2,1)S(1)} %copy.241, ...), channel_id=1, replica_groups=mesh['ctx'=8,'shard'=4] {'ctx'}, use_global_device_ids=true, to_apply=%region_39.40 | all-reduce | flops 7680 | bytes 30720 | tf_op jit(solution)/shard_map/psum | solution.py:416
  1332.1 42.3 %all-reduce.32.cloned.1.call-done = (bf16[192,1152]{0,1:T(8,128)(2,1)}, bf16[192,384]{0,1:T(8,128)(2,1)}, bf16[192,384]{1,0:T(8,128)(2,1)}, bf16[96,768]{1,0:T(8...) async-done(((bf16[192,1152]{0,1:T(8,128)(2,1)}, bf16[192,384]{0,1:T(8,128)(2,1)}, bf16[192,384]{1,0:T(8,128)(2,1)}, ...) | async-done | bytes 2211856 | tf_op jit(solution)/shard_map/psum | solution.py:415
  (708 shorter events, 582.0 us)
Async XLA Ops:
  7.2 45.5 %all-gather.7.cloned.1.call-start = ((), (), s32[]{:S(2)}) async-start(), calls=%async_computation.9 | async-start | bytes 2211840 | tf_op jit(solution)/shard_map/all_gather | solution.py:139
  7.9 202.5 %all-gather.9.cloned.1.call-start = ((), (), s32[]{:S(2)}) async-start(), calls=%async_computation.10 | async-start | bytes 14155776 | tf_op jit(solution)/shard_map/all_gather | solution.py:179
  59.5 272.5 %all-gather.11.cloned.1.call-start = ((), (), s32[]{:S(2)}) async-start(), calls=%async_computation.11 | async-start | bytes 2949120 | tf_op jit(solution)/shard_map/all_gather | solution.py:148
  60.3 304.9 %all-gather.13.cloned.1.call-start = ((), (), s32[]{:S(2)}) async-start(), calls=%async_computation.12 | async-start | bytes 2949120 | tf_op jit(solution)/shard_map/all_gather | solution.py:149
  61.1 116.2 %collective-permute-start.2 = (bf16[2,4,768]{2,1,0:T(4,128)(2,1)S(1)}, bf16[2,4,768]{2,1,0:T(4,128)(2,1)S(1)}, u32[]{:S(2)}, u32[]{:S(2)}) collective-permute-start(bf16[2,4,768]{2,1,0:T(4,128)(2,1)S(1)} %get-tuple-element.432), channel_id=1, source_target_pairs={{0,4},{4,8},{8,12},{12,16},{16,20},{20,24},{24,28},{1,5},{5,9},{9,... | collective-permute-start | bytes 36872 | tf_op jit(solution)/shard_map/ppermute | solution.py:24
  62.9 114.4 %collective-permute-start.3 = (bf16[2,4,768]{2,1,0:T(4,128)(2,1)S(1)}, bf16[2,4,768]{2,1,0:T(4,128)(2,1)S(1)}, u32[]{:S(2)}, u32[]{:S(2)}) collective-permute-start(bf16[2,4,768]{2,1,0:T(4,128)(2,1)S(1)} %get-tuple-element.433), channel_id=1, source_target_pairs={{4,0},{8,4},{12,8},{16,12},{20,16},{24,20},{28,24},{5,1},{9,5},{13... | collective-permute-start | bytes 36872 | tf_op jit(solution)/shard_map/ppermute | solution.py:27
  65.4 1000.9 %reduce-scatter.34.cloned.1.call-start = ((), (), s32[]{:S(2)}) async-start(), calls=%async_computation.21 | async-start | bytes 737280
  65.5 97.4 %copy-start.99 = (bf16[96,54]{0,1:T(8,128)(2,1)S(1)}, bf16[96,54]{0,1:T(8,128)(2,1)}, u32[]{:S(2)}) copy-start(bf16[96,54]{0,1:T(8,128)(2,1)} %param.24) | copy-start | bytes 31108
  79.3 353.1 %copy-start.63 = (f32[768]{0:T(1024)}, f32[768]{0:T(1024)S(1)}, u32[]{:S(2)}) copy-start(f32[768]{0:T(1024)S(1)} %convert_element_type.299) | copy-start | bytes 9220
  93.2 91.4 %copy-start.81 = (f32[768]{0:T(1024)}, f32[768]{0:T(1024)S(1)}, u32[]{:S(2)}) copy-start(f32[768]{0:T(1024)S(1)} %get-tuple-element.339) | copy-start | bytes 9220
  93.2 91.4 %copy-start.83 = (f32[768]{0:T(1024)}, f32[768]{0:T(1024)S(1)}, u32[]{:S(2)}) copy-start(f32[768]{0:T(1024)S(1)} %get-tuple-element.345) | copy-start | bytes 9220
  93.2 91.4 %copy-start.85 = (f32[768]{0:T(1024)}, f32[768]{0:T(1024)S(1)}, u32[]{:S(2)}) copy-start(f32[768]{0:T(1024)S(1)} %get-tuple-element.346) | copy-start | bytes 9220
  93.2 91.4 %copy-start.87 = (f32[768]{0:T(1024)}, f32[768]{0:T(1024)S(1)}, u32[]{:S(2)}) copy-start(f32[768]{0:T(1024)S(1)} %get-tuple-element.347) | copy-start | bytes 9220
  93.2 91.4 %copy-start.89 = (f32[768]{0:T(1024)}, f32[768]{0:T(1024)S(1)}, u32[]{:S(2)}) copy-start(f32[768]{0:T(1024)S(1)} %get-tuple-element.340) | copy-start | bytes 9220
  93.3 91.4 %copy-start.91 = (f32[768]{0:T(1024)}, f32[768]{0:T(1024)S(1)}, u32[]{:S(2)}) copy-start(f32[768]{0:T(1024)S(1)} %get-tuple-element.341) | copy-start | bytes 9220
  93.3 91.4 %copy-start.93 = (f32[768]{0:T(1024)}, f32[768]{0:T(1024)S(1)}, u32[]{:S(2)}) copy-start(f32[768]{0:T(1024)S(1)} %get-tuple-element.342) | copy-start | bytes 9220
  93.3 91.4 %copy-start.95 = (f32[768]{0:T(1024)}, f32[768]{0:T(1024)S(1)}, u32[]{:S(2)}) copy-start(f32[768]{0:T(1024)S(1)} %get-tuple-element.343) | copy-start | bytes 9220
  321.8 110.6 %copy-start.61 = (f32[2,512]{1,0:T(2,128)}, f32[2,512]{1,0:T(2,128)S(1)}, u32[]{:S(2)}) copy-start(f32[2,512]{1,0:T(2,128)S(1)} %broadcast_multiply_fusion.23) | copy-start | bytes 12292
  323.4 109.0 %copy-start.65 = (f32[2,512]{1,0:T(2,128)}, f32[2,512]{1,0:T(2,128)S(1)}, u32[]{:S(2)}) copy-start(f32[2,512]{1,0:T(2,128)S(1)} %add_rsqrt_fusion.1) | copy-start | bytes 12292
  445.3 530.2 %copy-start.51 = (bf16[384,54,1]{0,1,2:T(8,128)(2,1)S(1)}, bf16[384,54,1]{0,1,2:T(8,128)(2,1)}, u32[]{:S(2)}) copy-start(bf16[384,54,1]{0,1,2:T(8,128)(2,1)} %copy-done.50) | copy-start | bytes 124420
  473.0 21.0 %collective-permute-start.1 = (bf16[2,512,768]{1,2,0:T(8,128)(2,1)}, bf16[2,512,768]{1,2,0:T(8,128)(2,1)S(1)}, u32[]{:S(2)}, u32[]{:S(2)}) collective-permute-start(bf16[2,512,768]{1,2,0:T(8,128)(2,1)} %fusion.234), channel_id=1, source_target_pairs={{0,4},{4,8},{8,12},{12,16},{16,20},{20,24},{24,28},{28,0},{1,5},{5... | collective-permute-start | bytes 4718600 | tf_op jit(solution)/shard_map/while/body/eval_jaxpr/ppermute | solution.py:34
  473.0 37.9 %collective-permute-start = (bf16[2,512,768]{1,2,0:T(8,128)(2,1)}, bf16[2,512,768]{1,2,0:T(8,128)(2,1)}, u32[]{:S(2)}, u32[]{:S(2)}) collective-permute-start(bf16[2,512,768]{1,2,0:T(8,128)(2,1)} %copy.304), channel_id=1, source_target_pairs={{0,4},{4,8},{8,12},{12,16},{16,20},{20,24},{24,28},{28,0},{1,5},{5... | collective-permute-start | bytes 4718600 | tf_op jit(solution)/shard_map/while/body/eval_jaxpr/ppermute | solution.py:34
  539.3 21.0 %collective-permute-start.1 = (bf16[2,512,768]{1,2,0:T(8,128)(2,1)}, bf16[2,512,768]{1,2,0:T(8,128)(2,1)S(1)}, u32[]{:S(2)}, u32[]{:S(2)}) collective-permute-start(bf16[2,512,768]{1,2,0:T(8,128)(2,1)} %fusion.234), channel_id=1, source_target_pairs={{0,4},{4,8},{8,12},{12,16},{16,20},{20,24},{24,28},{28,0},{1,5},{5... | collective-permute-start | bytes 4718600 | tf_op jit(solution)/shard_map/while/body/eval_jaxpr/ppermute | solution.py:34
  541.2 36.0 %collective-permute-start = (bf16[2,512,768]{1,2,0:T(8,128)(2,1)}, bf16[2,512,768]{1,2,0:T(8,128)(2,1)}, u32[]{:S(2)}, u32[]{:S(2)}) collective-permute-start(bf16[2,512,768]{1,2,0:T(8,128)(2,1)} %copy.304), channel_id=1, source_target_pairs={{0,4},{4,8},{8,12},{12,16},{16,20},{20,24},{24,28},{28,0},{1,5},{5... | collective-permute-start | bytes 4718600 | tf_op jit(solution)/shard_map/while/body/eval_jaxpr/ppermute | solution.py:34
  605.7 21.0 %collective-permute-start.1 = (bf16[2,512,768]{1,2,0:T(8,128)(2,1)}, bf16[2,512,768]{1,2,0:T(8,128)(2,1)S(1)}, u32[]{:S(2)}, u32[]{:S(2)}) collective-permute-start(bf16[2,512,768]{1,2,0:T(8,128)(2,1)} %fusion.234), channel_id=1, source_target_pairs={{0,4},{4,8},{8,12},{12,16},{16,20},{20,24},{24,28},{28,0},{1,5},{5... | collective-permute-start | bytes 4718600 | tf_op jit(solution)/shard_map/while/body/eval_jaxpr/ppermute | solution.py:34
  606.7 36.9 %collective-permute-start = (bf16[2,512,768]{1,2,0:T(8,128)(2,1)}, bf16[2,512,768]{1,2,0:T(8,128)(2,1)}, u32[]{:S(2)}, u32[]{:S(2)}) collective-permute-start(bf16[2,512,768]{1,2,0:T(8,128)(2,1)} %copy.304), channel_id=1, source_target_pairs={{0,4},{4,8},{8,12},{12,16},{16,20},{20,24},{24,28},{28,0},{1,5},{5... | collective-permute-start | bytes 4718600 | tf_op jit(solution)/shard_map/while/body/eval_jaxpr/ppermute | solution.py:34
  672.0 21.0 %collective-permute-start.1 = (bf16[2,512,768]{1,2,0:T(8,128)(2,1)}, bf16[2,512,768]{1,2,0:T(8,128)(2,1)S(1)}, u32[]{:S(2)}, u32[]{:S(2)}) collective-permute-start(bf16[2,512,768]{1,2,0:T(8,128)(2,1)} %fusion.234), channel_id=1, source_target_pairs={{0,4},{4,8},{8,12},{12,16},{16,20},{20,24},{24,28},{28,0},{1,5},{5... | collective-permute-start | bytes 4718600 | tf_op jit(solution)/shard_map/while/body/eval_jaxpr/ppermute | solution.py:34
  672.1 37.8 %collective-permute-start = (bf16[2,512,768]{1,2,0:T(8,128)(2,1)}, bf16[2,512,768]{1,2,0:T(8,128)(2,1)}, u32[]{:S(2)}, u32[]{:S(2)}) collective-permute-start(bf16[2,512,768]{1,2,0:T(8,128)(2,1)} %copy.304), channel_id=1, source_target_pairs={{0,4},{4,8},{8,12},{12,16},{16,20},{20,24},{24,28},{28,0},{1,5},{5... | collective-permute-start | bytes 4718600 | tf_op jit(solution)/shard_map/while/body/eval_jaxpr/ppermute | solution.py:34
  738.4 21.0 %collective-permute-start.1 = (bf16[2,512,768]{1,2,0:T(8,128)(2,1)}, bf16[2,512,768]{1,2,0:T(8,128)(2,1)S(1)}, u32[]{:S(2)}, u32[]{:S(2)}) collective-permute-start(bf16[2,512,768]{1,2,0:T(8,128)(2,1)} %fusion.234), channel_id=1, source_target_pairs={{0,4},{4,8},{8,12},{12,16},{16,20},{20,24},{24,28},{28,0},{1,5},{5... | collective-permute-start | bytes 4718600 | tf_op jit(solution)/shard_map/while/body/eval_jaxpr/ppermute | solution.py:34
  738.4 37.9 %collective-permute-start = (bf16[2,512,768]{1,2,0:T(8,128)(2,1)}, bf16[2,512,768]{1,2,0:T(8,128)(2,1)}, u32[]{:S(2)}, u32[]{:S(2)}) collective-permute-start(bf16[2,512,768]{1,2,0:T(8,128)(2,1)} %copy.304), channel_id=1, source_target_pairs={{0,4},{4,8},{8,12},{12,16},{16,20},{20,24},{24,28},{28,0},{1,5},{5... | collective-permute-start | bytes 4718600 | tf_op jit(solution)/shard_map/while/body/eval_jaxpr/ppermute | solution.py:34
  804.7 21.0 %collective-permute-start.1 = (bf16[2,512,768]{1,2,0:T(8,128)(2,1)}, bf16[2,512,768]{1,2,0:T(8,128)(2,1)S(1)}, u32[]{:S(2)}, u32[]{:S(2)}) collective-permute-start(bf16[2,512,768]{1,2,0:T(8,128)(2,1)} %fusion.234), channel_id=1, source_target_pairs={{0,4},{4,8},{8,12},{12,16},{16,20},{20,24},{24,28},{28,0},{1,5},{5... | collective-permute-start | bytes 4718600 | tf_op jit(solution)/shard_map/while/body/eval_jaxpr/ppermute | solution.py:34
  804.7 37.9 %collective-permute-start = (bf16[2,512,768]{1,2,0:T(8,128)(2,1)}, bf16[2,512,768]{1,2,0:T(8,128)(2,1)}, u32[]{:S(2)}, u32[]{:S(2)}) collective-permute-start(bf16[2,512,768]{1,2,0:T(8,128)(2,1)} %copy.304), channel_id=1, source_target_pairs={{0,4},{4,8},{8,12},{12,16},{16,20},{20,24},{24,28},{28,0},{1,5},{5... | collective-permute-start | bytes 4718600 | tf_op jit(solution)/shard_map/while/body/eval_jaxpr/ppermute | solution.py:34
  871.0 21.0 %collective-permute-start.1 = (bf16[2,512,768]{1,2,0:T(8,128)(2,1)}, bf16[2,512,768]{1,2,0:T(8,128)(2,1)S(1)}, u32[]{:S(2)}, u32[]{:S(2)}) collective-permute-start(bf16[2,512,768]{1,2,0:T(8,128)(2,1)} %fusion.234), channel_id=1, source_target_pairs={{0,4},{4,8},{8,12},{12,16},{16,20},{20,24},{24,28},{28,0},{1,5},{5... | collective-permute-start | bytes 4718600 | tf_op jit(solution)/shard_map/while/body/eval_jaxpr/ppermute | solution.py:34
  871.0 37.9 %collective-permute-start = (bf16[2,512,768]{1,2,0:T(8,128)(2,1)}, bf16[2,512,768]{1,2,0:T(8,128)(2,1)}, u32[]{:S(2)}, u32[]{:S(2)}) collective-permute-start(bf16[2,512,768]{1,2,0:T(8,128)(2,1)} %copy.304), channel_id=1, source_target_pairs={{0,4},{4,8},{8,12},{12,16},{16,20},{20,24},{24,28},{28,0},{1,5},{5... | collective-permute-start | bytes 4718600 | tf_op jit(solution)/shard_map/while/body/eval_jaxpr/ppermute | solution.py:34
  937.4 21.0 %collective-permute-start.1 = (bf16[2,512,768]{1,2,0:T(8,128)(2,1)}, bf16[2,512,768]{1,2,0:T(8,128)(2,1)S(1)}, u32[]{:S(2)}, u32[]{:S(2)}) collective-permute-start(bf16[2,512,768]{1,2,0:T(8,128)(2,1)} %fusion.234), channel_id=1, source_target_pairs={{0,4},{4,8},{8,12},{12,16},{16,20},{20,24},{24,28},{28,0},{1,5},{5... | collective-permute-start | bytes 4718600 | tf_op jit(solution)/shard_map/while/body/eval_jaxpr/ppermute | solution.py:34
  937.4 37.9 %collective-permute-start = (bf16[2,512,768]{1,2,0:T(8,128)(2,1)}, bf16[2,512,768]{1,2,0:T(8,128)(2,1)}, u32[]{:S(2)}, u32[]{:S(2)}) collective-permute-start(bf16[2,512,768]{1,2,0:T(8,128)(2,1)} %copy.304), channel_id=1, source_target_pairs={{0,4},{4,8},{8,12},{12,16},{16,20},{20,24},{24,28},{28,0},{1,5},{5... | collective-permute-start | bytes 4718600 | tf_op jit(solution)/shard_map/while/body/eval_jaxpr/ppermute | solution.py:34
  1015.1 2.9 collective-permute-start.4
  1016.4 3.1 collective-permute-start.5
  1023.9 71.0 %reduce-scatter.28.cloned.1.call-start = ((), (), s32[]{:S(2)}) async-start(), calls=%async_computation.18 | async-start | bytes 2211840
  1036.8 81.6 %reduce-scatter.20.cloned.1.call-start = ((), (), s32[]{:S(2)}) async-start(), calls=%async_computation.14 | async-start | bytes 737280 | tf_op jit(solution)/shard_map/reduce_scatter | solution.py:389
  1038.5 102.6 %reduce-scatter.22.cloned.1.call-start = ((), (), s32[]{:S(2)}) async-start(), calls=%async_computation.15 | async-start | bytes 737280 | tf_op jit(solution)/shard_map/reduce_scatter | solution.py:392
  1042.1 122.4 %reduce-scatter.18.cloned.1.call-start = ((), (), s32[]{:S(2)}) async-start(), calls=%async_computation.13 | async-start | bytes 737280 | tf_op jit(solution)/shard_map/reduce_scatter | solution.py:380
  1045.9 167.3 %reduce-scatter.26.cloned.1.call-start = ((), (), s32[]{:S(2)}) async-start(), calls=%async_computation.17 | async-start | bytes 2949120 | tf_op jit(solution)/shard_map/reduce_scatter | solution.py:404
  1054.2 208.9 %reduce-scatter.24.cloned.1.call-start = ((), (), s32[]{:S(2)}) async-start(), calls=%async_computation.16 | async-start | bytes 2949120 | tf_op jit(solution)/shard_map/reduce_scatter | solution.py:401
  1060.9 236.9 %reduce-scatter.30.cloned.1.call-start = ((), (), s32[]{:S(2)}) async-start(), calls=%async_computation.19 | async-start | bytes 245760
  1062.0 243.0 %reduce-scatter.32.cloned.1.call-start = ((), (), s32[]{:S(2)}) async-start(), calls=%async_computation.20 | async-start | bytes 122880
  1064.1 199.1 %copy-start.42 = (bf16[2,512,384]{2,1,0:T(8,128)(2,1)S(1)}, bf16[2,512,384]{2,1,0:T(8,128)(2,1)}, u32[]{:S(2)}) copy-start(bf16[2,512,384]{2,1,0:T(8,128)(2,1)} %copy-done.41) | copy-start | bytes 2359300
  1064.9 309.6 %all-reduce.32.cloned.1.call-start = ((), (), s32[]{:S(2)}) async-start(), calls=%async_computation.22 | async-start | bytes 4816896 | tf_op jit(solution)/shard_map/psum | solution.py:415
  (130 other events, 1208.5 us)
Sparse Core Ops, SparseCore 0:
  9.6 43.0 all-gather.6
  59.6 70.9 all-gather.8
  132.2 57.2 all-gather.10
  191.5 49.2 all-gather.12
  1024.0 31.8 reduce-scatter.33
  1058.1 36.7 reduce-scatter.27
  1097.3 21.0 reduce-scatter.19
  1120.8 20.2 reduce-scatter.21
  1144.0 20.3 reduce-scatter.17
  1166.7 46.3 reduce-scatter.25
  1215.6 47.5 reduce-scatter.23
  1265.9 18.9 reduce-scatter.29
  1287.7 17.2 reduce-scatter.31
  1310.7 63.6 all-reduce.31
where the time goes:
time: 1400 us; the launch traced here: 1390 us
  waiting for transfers between devices  513 us (37%)
  matrix products  372 us (27%)
  local copies, waits for them, and re-layouts  173 us (12%)
  blocking collectives  147 us (10%)
  other arithmetic  143 us (10%)
  starting transfers between devices  24.6 us (2%)
  between operations  17.3 us (1%)
    ppermute x16, waiting for transfers between devices, shifted(): lax.ppermute(value, axis, [(i, (i + by) % devices) for i in range(devices)])  224 us
    dot_general x8, matrix products, attend_back(): jnp.einsum('sqhe,skhe->sqhk', grad_four, values_four, preferred_element_t...  62.3 us
    reduce_scatter x1, waiting for transfers between devices, shards(): lax.psum_scatter(grad_ffn_inner.astype(jnp.bfloat16), 'shard', scatter_di...  50 us
    while x120, local copies, waits for them, and re-layouts  49.7 us
    reduce_scatter x1, waiting for transfers between devices, shards(): lax.psum_scatter(grad_ffn_outer.astype(jnp.bfloat16), 'shard', scatter_di...  48.7 us
    dot_general x8, matrix products, attend_back(): jnp.einsum('sqhk,sqhe->skhe', d_scores, query_four, preferred_element_typ...  47.6 us
    all_gather x1, waiting for transfers between devices, shards(): lax.all_gather(qkv_weight, 'shard', axis=0, tiled=True)  44.7 us
    dot_general x8, matrix products, attend_back(): jnp.einsum('sqhk,skhe->sqhe', d_scores, keys_four, preferred_element_type...  43.7 us
  transfers between devices with their start and end apart: 34, of which 26 were waited for; matrix products, arithmetic and copies ran while one was open for 21% of the time, Pallas kernels for 0%

commit v1 on v0

--- a/solution.py
+++ b/solution.py
@@ -1,9 +1,12 @@
+import functools
 from functools import partial
 import math
 
 import jax
 import jax.numpy as jnp
 from jax import lax
+from jax.experimental import pallas as pl
+from jax.experimental.pallas import tpu as pltpu
 from jax.sharding import PartitionSpec as P
 
 D = 768
@@ -27,11 +30,6 @@
         high = lax.ppermute(lax.slice_in_dim(block, 0, width, axis=dim), axis, backward)
         block = jnp.concatenate([low, block, high], axis=dim)
     return block
-
-
-def shifted(value, axis, by):
-    devices = lax.axis_size(axis)
-    return lax.ppermute(value, axis, [(i, (i + by) % devices) for i in range(devices)])
 
 
 def layer_norm(hidden, norm_gain, norm_bias):
@@ -57,62 +55,398 @@
     return values.reshape(values.shape[0], values.shape[1], HEADS, HEAD)
 
 
-def attend_fold(query_four, running, shard_piece):
-    attn_width = HEADS * HEAD
-    piece_rows = shard_piece.shape[1]
-    step_rows = math.gcd(piece_rows, 256)
-    score_scale = 1.0 / math.sqrt(HEAD)
-
-    def key_step(step_index, current):
-        row_top, row_total, weighted = current
-        key_block = lax.dynamic_slice_in_dim(shard_piece, step_index * step_rows, step_rows, 1)
-        keys_four = four_heads(key_block[..., :attn_width])
-        values_four = four_heads(key_block[..., attn_width:])
-        scores = (
-            jnp.einsum("sqhe,skhe->sqhk", query_four, keys_four, preferred_element_type=jnp.float32)
-            * score_scale
-        )
-        new_top = jnp.maximum(row_top, jnp.max(scores, axis=-1))
-        exp_scores = jnp.exp(scores - new_top[..., None])
-        rescale = jnp.exp(row_top - new_top)
-        row_total = row_total * rescale + jnp.sum(exp_scores, axis=-1)
-        weighted = weighted * rescale[..., None] + jnp.einsum(
-            "sqhk,skhe->sqhe",
-            exp_scores.astype(jnp.bfloat16),
-            values_four,
-            preferred_element_type=jnp.float32,
-        )
-        return (new_top, row_total, weighted)
-
-    return lax.fori_loop(0, piece_rows // step_rows, key_step, running)
-
-
-def attend_back(query_four, grad_four, row_lse, row_delta, keys_four, values_four):
-    score_scale = 1.0 / math.sqrt(HEAD)
-    scores = (
-        jnp.einsum("sqhe,skhe->sqhk", query_four, keys_four, preferred_element_type=jnp.float32)
-        * score_scale
-    )
-    attend_probs = jnp.exp(scores - row_lse[..., None])
-    d_probs = jnp.einsum(
-        "sqhe,skhe->sqhk", grad_four, values_four, preferred_element_type=jnp.float32
-    )
-    d_scores = (attend_probs * (d_probs - row_delta[..., None])).astype(jnp.bfloat16)
-    d_query = (
-        jnp.einsum("sqhk,skhe->sqhe", d_scores, keys_four, preferred_element_type=jnp.float32)
-        * score_scale
-    )
-    d_key = (
-        jnp.einsum("sqhk,sqhe->skhe", d_scores, query_four, preferred_element_type=jnp.float32)
-        * score_scale
-    )
-    d_value = jnp.einsum(
-        "sqhk,sqhe->skhe",
-        attend_probs.astype(jnp.bfloat16),
-        grad_four,
-        preferred_element_type=jnp.float32,
-    )
-    return (d_query, d_key, d_value)
+BF = jnp.bfloat16
+F32 = jnp.float32
+MESH_ID = pl.DeviceIdType.MESH
+NT = (((1,), (1,)), ((), ()))
+NN = (((1,), (0,)), ((), ()))
+EXP2_SCALE = math.log2(math.e) / math.sqrt(HEAD)
+TRIPLE = 3
+QUADS = 4
+CHUNK = 128
+
+
+def dot(a, b, dims):
+    return lax.dot_general(a, b, dims, preferred_element_type=F32)
+
+
+def swap_halves(packed):
+    return jnp.concatenate([packed[:, HEAD:], packed[:, :HEAD]], axis=1)
+
+
+def low_lanes():
+    return lax.broadcasted_iota(jnp.int32, (1, 2 * HEAD), 1) < HEAD
+
+
+def remote(src, dst, send, recv, target):
+    return pltpu.make_async_remote_copy(
+        src_ref=src, dst_ref=dst, send_sem=send, recv_sem=recv,
+        device_id=target, device_id_type=MESH_ID,
+    )
+
+
+def greet(peers):
+    barrier = pltpu.get_barrier_semaphore()
+    for peer in peers:
+        pl.semaphore_signal(barrier, inc=1, device_id=peer, device_id_type=MESH_ID)
+    pl.semaphore_wait(barrier, len(peers))
+
+
+def attend_forward_kernel(
+    members, kv_in, q_in, kv_all, q_all, out_all, lse, ctx_out,
+    out_send, kv_s, kv_r, q_s, q_r, f_s, f_r, o_s, o_r, local,
+):
+    rows = kv_in.shape[2]
+    half = rows // 2
+    me = lax.axis_index("ctx")
+    shard = lax.axis_index("shard")
+    quad, sub = me // members, me % members
+
+    def peer(step):
+        return ((quad + step) % QUADS * members + sub, shard)
+
+    def sibling(step):
+        return (quad * members + (sub + step) % members, shard)
+
+    greet([peer(k) for k in range(1, QUADS)] + [sibling(m) for m in range(1, members)])
+
+    def kv_copy(h, k):
+        return remote(
+            kv_in.at[(quad + k) % QUADS, h], kv_all.at[h, quad, sub], kv_s.at[h, k], kv_r.at[h, k], peer(k)
+        )
+
+    def q_copy(h, k):
+        return remote(
+            q_in.at[(quad + k) % QUADS, h], q_all.at[h, quad], q_s.at[h, k], q_r.at[h, k], peer(k)
+        )
+
+    def forward_copy(h, m):
+        return remote(
+            kv_all.at[h, :, sub], kv_all.at[h, :, sub], f_s.at[h, m], f_r.at[h, m], sibling(m)
+        )
+
+    def out_copy(h, i, k):
+        return remote(
+            out_send.at[h, i], ctx_out.at[quad, h], o_s.at[h, i], o_r.at[h, i], peer(k)
+        )
+
+    own_kv = pltpu.make_async_copy(kv_in.at[quad], kv_all.at[:, quad, sub], local.at[0])
+    own_q = pltpu.make_async_copy(q_in.at[quad], q_all.at[:, quad], local.at[1])
+    own_kv.start()
+    own_q.start()
+    for h in range(TRIPLE):
+        for k in range(1, QUADS):
+            kv_copy(h, k).start()
+            q_copy(h, k).start()
+    own_kv.wait()
+    own_q.wait()
+
+    def receive(h):
+        for k in range(1, QUADS):
+            kv_copy(h, k).wait_recv()
+            q_copy(h, k).wait_recv()
+        for m in range(1, members):
+            forward_copy(h, m).start()
+
+    receive(0)
+    is_low = low_lanes()
+
+    def block(step, carry):
+        h, i = step // QUADS, step % QUADS
+        k = (i + 1) % QUADS
+        source = (quad + k) % QUADS
+
+        @pl.when(i == 0)
+        def _():
+            for m in range(1, members):
+                forward_copy(h, m).wait_recv()
+
+        keys = kv_all[h].reshape(QUADS * members * rows, 2 * HEAD)
+
+        def rows_turn(r, inner):
+            at = pl.multiple_of(r * CHUNK, CHUNK)
+            packed = q_all[h, source, pl.ds(at, CHUNK), :]
+            outs = []
+            stats = []
+            for part in range(2):
+                q = jnp.where(is_low, packed if part == 0 else swap_halves(packed), jnp.zeros_like(packed))
+                scores = dot(q, keys, NT)
+                top = jnp.max(scores, axis=1, keepdims=True)
+                probs = jnp.exp2((scores - top) * EXP2_SCALE)
+                total = jnp.sum(probs, axis=1, keepdims=True)
+                outs.append(dot(probs.astype(BF), keys, NN) / total)
+                stats.append(top * EXP2_SCALE + jnp.log2(total))
+            both = jnp.where(is_low, swap_halves(outs[0]), outs[1])
+            out_all[h, source, pl.ds(at, CHUNK), :] = both
+            out_send[h, i, pl.ds(at, CHUNK), :] = both.astype(BF)
+            for part in range(2):
+                lse[h, source, part, r] = jnp.broadcast_to(stats[part], (CHUNK, CHUNK)).T[0:8, :]
+            return inner
+
+        lax.fori_loop(0, half // CHUNK, rows_turn, 0)
+
+        @pl.when(k != 0)
+        def _():
+            out_copy(h, i, k).start()
+
+        @pl.when(k == 0)
+        def _():
+            own = pltpu.make_async_copy(out_send.at[h, i], ctx_out.at[quad, h], local.at[0])
+            own.start()
+            own.wait()
+
+        @pl.when((i == 2) & (h < TRIPLE - 1))
+        def _():
+            receive(h + 1)
+
+        return carry
+
+    lax.fori_loop(0, TRIPLE * QUADS, block, 0)
+    for h in range(TRIPLE):
+        for k in range(1, QUADS):
+            out_copy(h, k - 1, k).wait()
+            kv_copy(h, k).wait_send()
+            q_copy(h, k).wait_send()
+        for m in range(1, members):
+            forward_copy(h, m).wait_send()
+
+
+def attend_forward(kv, q, members):
+    rows = kv.shape[2]
+    half = rows // 2
+    vm = pl.BlockSpec(memory_space=pltpu.VMEM)
+    anywhere = pl.BlockSpec(memory_space=pl.ANY)
+    dma = pltpu.SemaphoreType.DMA
+    total = TRIPLE * QUADS * rows * QUADS * members * rows
+    return pl.pallas_call(
+        functools.partial(attend_forward_kernel, members),
+        in_specs=[anywhere, anywhere],
+        out_specs=[vm, vm, vm, vm, anywhere],
+        out_shape=[
+            jax.ShapeDtypeStruct((TRIPLE, QUADS, members, rows, 2 * HEAD), BF),
+            jax.ShapeDtypeStruct((TRIPLE, QUADS, half, 2 * HEAD), BF),
+            jax.ShapeDtypeStruct((TRIPLE, QUADS, half, 2 * HEAD), F32),
+            jax.ShapeDtypeStruct((TRIPLE, QUADS, 2, half // CHUNK, 8, CHUNK), F32),
+            jax.ShapeDtypeStruct((QUADS, TRIPLE, half, 2 * HEAD), BF),
+        ],
+        scratch_shapes=[
+            pltpu.VMEM((TRIPLE, QUADS, half, 2 * HEAD), BF),
+            dma((TRIPLE, QUADS)), dma((TRIPLE, QUADS)), dma((TRIPLE, QUADS)), dma((TRIPLE, QUADS)),
+            dma((TRIPLE, members)), dma((TRIPLE, members)), dma((TRIPLE, QUADS)), dma((TRIPLE, QUADS)),
+            dma((2,)),
+        ],
+        compiler_params=pltpu.CompilerParams(
+            collective_id=1, has_side_effects=True, vmem_limit_bytes=56 * 2**20
+        ),
+        cost_estimate=pl.CostEstimate(flops=total * 256, bytes_accessed=8 * 2**20, transcendentals=total),
+    )(kv, q)
+
+
+def attend_backward_kernel(
+    members, d_in, kv_all, q_all, out_all, lse, dq_out, dkv_out,
+    d_all, q_zero, d_zero, stat, delta, dq_sum, dkv_sum, own_part, sib_send, sib_recv, dkv_send, dq_send,
+    d_s, d_r, p_s, p_r, k_s, k_r, g_s, g_r, local,
+):
+    rows = kv_all.shape[3]
+    half = rows // 2
+    me = lax.axis_index("ctx")
+    shard = lax.axis_index("shard")
+    quad, sub = me // members, me % members
+    steps = TRIPLE * QUADS
+
+    def peer(step):
+        return ((quad + step) % QUADS * members + sub, shard)
+
+    def sibling(step):
+        return (quad * members + (sub + step) % members, shard)
+
+    greet([peer(k) for k in range(1, QUADS)] + [sibling(m) for m in range(1, members)])
+
+    def d_copy(h, k):
+        return remote(
+            d_in.at[(quad + k) % QUADS, h], d_all.at[h, quad], d_s.at[h, k], d_r.at[h, k], peer(k)
+        )
+
+    def part_copy(step, m):
+        return remote(
+            sib_send.at[step % 2, m], sib_recv.at[step, m], p_s.at[step, m], p_r.at[step, m], sibling(m)
+        )
+
+    def dkv_copy(h, i, k):
+        return remote(
+            dkv_send.at[h, i], dkv_out.at[quad, h], k_s.at[h, i], k_r.at[h, i], peer(k)
+        )
+
+    def dq_copy(h, k):
+        return remote(
+            dq_send.at[h, (quad + k) % QUADS], dq_out.at[quad, h], g_s.at[h, k], g_r.at[h, k], peer(k)
+        )
+
+    own = pltpu.make_async_copy(d_in.at[quad], d_all.at[:, quad], local.at[0])
+    own.start()
+    for h in range(TRIPLE):
+        for k in range(1, QUADS):
+            d_copy(h, k).start()
+    own.wait()
+    is_low = low_lanes()
+
+    def finish(step):
+        h, i = step // QUADS, step % QUADS
+        k = (i + 1) % QUADS
+        total = own_part[step % 2]
+        for m in range(1, members):
+            part_copy(step, m).wait_recv()
+            total = total + sib_recv[step, m].astype(F32)
+        dkv_send[h, i] = total.astype(BF)
+
+        @pl.when(k != 0)
+        def _():
+            dkv_copy(h, i, k).start()
+
+        @pl.when(k == 0)
+        def _():
+            own = pltpu.make_async_copy(dkv_send.at[h, i], dkv_out.at[quad, h], local.at[0])
+            own.start()
+            own.wait()
+
+    def block(step, carry):
+        h, i = step // QUADS, step % QUADS
+        k = (i + 1) % QUADS
+        source = (quad + k) % QUADS
+
+        @pl.when(i == 0)
+        def _():
+            for j in range(1, QUADS):
+                d_copy(h, j).wait_recv()
+
+            def prepare(b, inner):
+                q = q_all[h, b]
+                d = d_all[h, b]
+                zero = jnp.zeros_like(q)
+                q_zero[b, 0:half] = jnp.where(is_low, q, zero)
+                q_zero[b, half:rows] = jnp.where(is_low, swap_halves(q), zero)
+                d_zero[b, 0:half] = jnp.where(is_low, zero, swap_halves(d))
+                d_zero[b, half:rows] = jnp.where(is_low, zero, d)
+                both = (out_all[h, b] * d.astype(F32)).T
+                delta[b, :, 0:half] = jnp.broadcast_to(jnp.sum(both[0:HEAD], axis=0, keepdims=True), (8, half))
+                delta[b, :, half:rows] = jnp.broadcast_to(jnp.sum(both[HEAD:], axis=0, keepdims=True), (8, half))
+                for part in range(2):
+                    for r in range(half // CHUNK):
+                        at = part * half + r * CHUNK
+                        stat[b, :, at : at + CHUNK] = lse[h, b, part, r]
+                dq_sum[b] = jnp.zeros((HEAD, rows), F32)
+                return inner
+
+            lax.fori_loop(0, QUADS, prepare, 0)
+
+        keys = kv_all[h, source].reshape(members * rows, 2 * HEAD)
+        keys_turned = keys.T[0:HEAD]
+        dkv_sum[...] = jnp.zeros_like(dkv_sum)
+
+        def queries_turn(b, inner):
+            qz = q_zero[b]
+            dz = d_zero[b]
+            probs = jnp.exp2(dot(keys, qz, NT) * EXP2_SCALE - stat[b, 0:1, :])
+            d_probs = dot(keys, dz, NT)
+            d_scores = (probs * (d_probs - delta[b, 0:1, :])).astype(BF)
+            dkv_sum[...] += dot(d_scores, qz, NN) * (1.0 / math.sqrt(HEAD)) + dot(probs.astype(BF), dz, NN)
+            dq_sum[b] += dot(keys_turned, d_scores, NN)
+            return inner
+
+        lax.fori_loop(0, QUADS, queries_turn, 0)
+
+        @pl.when(step > 0)
+        def _():
+            finish(step - 1)
+
+        own_part[step % 2] = dkv_sum[pl.ds(pl.multiple_of(sub * rows, rows), rows), :]
+        for m in range(1, members):
+            @pl.when(step > 1)
+            def _():
+                part_copy(step - 2, m).wait_send()
+            target = (sub + m) % members
+            sib_send[step % 2, m] = dkv_sum[pl.ds(pl.multiple_of(target * rows, rows), rows), :].astype(BF)
+            part_copy(step, m).start()
+
+        @pl.when(i == QUADS - 1)
+        def _():
+            def give(b, inner):
+                turned = dq_sum[b] * (1.0 / math.sqrt(HEAD))
+                dq_send[h, b] = jnp.concatenate([turned[:, 0:half], turned[:, half:rows]], axis=0).T.astype(BF)
+                return inner
+
+            lax.fori_loop(0, QUADS, give, 0)
+            for j in range(1, QUADS):
+                dq_copy(h, j).start()
+            mine = pltpu.make_async_copy(dq_send.at[h, quad], dq_out.at[quad, h], local.at[0])
+            mine.start()
+            mine.wait()
+
+        return carry
+
+    lax.fori_loop(0, steps, block, 0)
+    finish(steps - 1)
+    for m in range(1, members):
+        part_copy(steps - 2, m).wait_send()
+        part_copy(steps - 1, m).wait_send()
+    for h in range(TRIPLE):
+        for k in range(1, QUADS):
+            d_copy(h, k).wait_send()
+            dkv_copy(h, k - 1, k).wait()
+            dq_copy(h, k).wait()
+
+
+def attend_backward(d_context, kv_all, q_all, out_all, lse, members):
+    rows = kv_all.shape[3]
+    half = rows // 2
+    steps = TRIPLE * QUADS
+    vm = pl.BlockSpec(memory_space=pltpu.VMEM)
+    anywhere = pl.BlockSpec(memory_space=pl.ANY)
+    dma = pltpu.SemaphoreType.DMA
+    total = TRIPLE * QUADS * rows * QUADS * members * rows
+    return pl.pallas_call(
+        functools.partial(attend_backward_kernel, members),
+        in_specs=[anywhere, vm, vm, vm, vm],
+        out_specs=[anywhere, anywhere],
+        out_shape=[
+            jax.ShapeDtypeStruct((QUADS, TRIPLE, half, 2 * HEAD), BF),
+            jax.ShapeDtypeStruct((QUADS, TRIPLE, rows, 2 * HEAD), BF),
+        ],
+        scratch_shapes=[
+            pltpu.VMEM((TRIPLE, QUADS, half, 2 * HEAD), BF),
+            pltpu.VMEM((QUADS, rows, 2 * HEAD), BF),
+            pltpu.VMEM((QUADS, rows, 2 * HEAD), BF),
+            pltpu.VMEM((QUADS, 8, rows), F32),
+            pltpu.VMEM((QUADS, 8, rows), F32),
+            pltpu.VMEM((QUADS, HEAD, rows), F32),
+            pltpu.VMEM((members * rows, 2 * HEAD), F32),
+            pltpu.VMEM((2, rows, 2 * HEAD), F32),
+            pltpu.VMEM((2, members, rows, 2 * HEAD), BF),
+            pltpu.VMEM((steps, members, rows, 2 * HEAD), BF),
+            pltpu.VMEM((TRIPLE, QUADS, rows, 2 * HEAD), BF),
+            pltpu.VMEM((TRIPLE, QUADS, half, 2 * HEAD), BF),
+            dma((TRIPLE, QUADS)), dma((TRIPLE, QUADS)),
+            dma((steps, members)), dma((steps, members)),
+            dma((TRIPLE, QUADS)), dma((TRIPLE, QUADS)), dma((TRIPLE, QUADS)), dma((TRIPLE, QUADS)),
+            dma((2,)),
+        ],
+        compiler_params=pltpu.CompilerParams(
+            collective_id=2, has_side_effects=True, vmem_limit_bytes=56 * 2**20
+        ),
+        cost_estimate=pl.CostEstimate(flops=total * 640, bytes_accessed=8 * 2**20, transcendentals=total),
+    )(d_context, kv_all, q_all, out_all, lse)
+
+
+def pack_heads(values):
+    seqs, rows, _ = values.shape
+    split = values.reshape(seqs, 2, rows // 2, HEADS, HEAD)
+    return split.transpose(0, 3, 2, 1, 4).reshape(QUADS, TRIPLE, rows // 2, 2 * HEAD)
+
+
+def unpack_heads(packed, seqs):
+    half = packed.shape[2]
+    split = packed.reshape(seqs, HEADS, half, 2, HEAD)
+    return split.transpose(0, 3, 2, 1, 4).reshape(seqs, 2 * half, HEADS * HEAD)
 
 
 def shards(
@@ -169,18 +503,11 @@
     mixed_qkv = jnp.einsum("sti,io->sto", hidden_in, full_qkv, preferred_element_type=jnp.float32)
     query_low = mixed_qkv[..., :attn_width].astype(jnp.bfloat16)
     pair_low = mixed_qkv[..., attn_width:].astype(jnp.bfloat16)
-    query_four = four_heads(query_low)
-    start_state = (
-        jnp.full((seq_count, local_rows, HEADS), -jnp.inf, jnp.float32),
-        jnp.zeros((seq_count, local_rows, HEADS), jnp.float32),
-        jnp.zeros((seq_count, local_rows, HEADS, HEAD), jnp.float32),
-    )
-    row_top, row_total, weighted = attend_fold(
-        query_four, start_state, lax.all_gather(pair_low, "ctx", axis=1, tiled=True)
-    )
-    row_lse = row_top + jnp.log(row_total)
-    context = weighted / row_total[..., None]
-    context_low = context.reshape(seq_count, local_rows, attn_width).astype(jnp.bfloat16)
+    members = lax.axis_size("ctx") // QUADS
+    pair = pair_low.reshape(seq_count, local_rows, 2, HEADS, HEAD).transpose(0, 3, 1, 2, 4)
+    pair = pair.reshape(QUADS, TRIPLE, local_rows, 2 * HEAD)
+    kv_all, q_all, out_all, lse, context_packed = attend_forward(pair, pack_heads(query_low), members)
+    context_low = unpack_heads(context_packed, seq_count)
     depth_fwd = full_depth.astype(jnp.float32)
     spread = rows_ext[:, 0:local_rows].astype(jnp.float32) * depth_fwd[0]
     for offset in range(1, KERNEL):
@@ -325,42 +652,10 @@
     grad_conv_value = jnp.einsum(
         "sti,sta->ia", hidden_in, d_value_low, preferred_element_type=jnp.float32
     )
-    grad_four = four_heads(d_context_low)
-    row_delta = jnp.sum(grad_four.astype(jnp.float32) * context, axis=-1)
-
-    def keys_turn(step_index, current):
-        packet, grad_pack, query_sum = current
-        d_query, d_key, d_value = attend_back(
-            query_four,
-            grad_four,
-            row_lse,
-            row_delta,
-            four_heads(packet[..., :attn_width]),
-            four_heads(packet[..., attn_width:]),
-        )
-        grad_pack = grad_pack + jnp.concatenate(
-            [
-                d_key.reshape(seq_count, local_rows, attn_width),
-                d_value.reshape(seq_count, local_rows, attn_width),
-            ],
-            axis=-1,
-        )
-        packet = shifted(packet, "ctx", 1)
-        grad_pack = shifted(grad_pack.astype(jnp.bfloat16), "ctx", 1).astype(grad_pack.dtype)
-        return (packet, grad_pack, query_sum + d_query)
-
-    finished = lax.fori_loop(
-        0,
-        lax.axis_size("ctx"),
-        keys_turn,
-        (
-            pair_low,
-            jnp.zeros((seq_count, local_rows, 2 * attn_width), jnp.float32),
-            jnp.zeros((seq_count, local_rows, HEADS, HEAD), jnp.float32),
-        ),
-    )
-    d_query_attn = finished[2].reshape(seq_count, local_rows, attn_width)
-    d_pair = finished[1]
+    dq_packed, dkv = attend_backward(pack_heads(d_context_low), kv_all, q_all, out_all, lse, members)
+    d_query_attn = unpack_heads(dq_packed, seq_count).astype(jnp.float32)
+    d_pair = dkv.reshape(seq_count, HEADS, local_rows, 2, HEAD).transpose(0, 2, 3, 1, 4)
+    d_pair = d_pair.reshape(seq_count, local_rows, 2 * attn_width)
     d_query_low = (d_query_attn + d_query_conv).astype(jnp.bfloat16)
     d_all_low = jnp.concatenate([d_query_low, d_pair.astype(jnp.bfloat16)], axis=-1)
     grad_qkv = jnp.einsum("sti,sto->io", hidden_in, d_all_low, preferred_element_type=jnp.float32)

time: 1400 us -> 912 us (0.65)
  waiting for transfers between devices: 513 us -> 236 us
  matrix products: 372 us -> 135 us
  Pallas kernels: 0 us -> 162 us
  other arithmetic: 143 us -> 67.8 us
  local copies, waits for them, and re-layouts: 173 us -> 112 us
  blocking collectives: 147 us -> 168 us
  starting transfers between devices: 24.6 us -> 8.51 us
    dot_general x72 -> x0, matrix products: 235 us -> none  [the longest x8 62.3 us: attend_back(): jnp.einsum('sqhe,skhe->sqhk', grad_four, values_four, preferred_element_t...]
    ppermute x16 -> x0, waiting for transfers between devices: 224 us -> none  [shifted(): lax.ppermute(value, axis, [(i, (i + by) % devices) for i in range(devices)])]
    pallas_call x0 -> x2, Pallas kernels: none -> 162 us  [the longest x1 94.1 us: attend_backward(): pl.pallas_call(functools.partial(attend_backward_kernel, members), in_spe...]
    while x121 -> x0, local copies, waits for them, and re-layouts: 53.2 us -> none
    convert_element_type x17 -> x0, other arithmetic: 52.5 us -> none  [the longest x8 33.7 us: keys_turn(): grad_pack.astype(jnp.bfloat16)]
    all_gather x1, waiting for transfers between devices: 44.7 us -> 0.02 us  [shards(): lax.all_gather(qkv_weight, 'shard', axis=0, tiled=True)]
    slice x24 -> x0, local copies, waits for them, and re-layouts: 38.7 us -> none  [the longest x8 19.3 us: keys_turn(): packet[..., attn_width:]]
    ppermute x16 -> x0, starting transfers between devices: 18.3 us -> none  [shifted(): lax.ppermute(value, axis, [(i, (i + by) % devices) for i in range(devices)])]
  transfers between devices with their start and end apart: 34 -> 17, of which waited for: 26 -> 9; matrix products, arithmetic and copies ran while one was open for 21% -> 19% of each run, Pallas kernels for 0% -> 7%
where the time goes in v1:
time: 912 us; the launch traced here: 908 us
  waiting for transfers between devices  236 us (26%)
  blocking collectives  168 us (18%)
  Pallas kernels  162 us (18%)
  matrix products  135 us (15%)
  local copies, waits for them, and re-layouts  112 us (12%)
  other arithmetic  67.8 us (7%)
  between operations  17.3 us (2%)
    pallas_call x1, Pallas kernels, attend_backward(): pl.pallas_call(functools.partial(attend_backward_kernel, members), in_spe...  94.1 us
    pallas_call x1, Pallas kernels, attend_forward(): pl.pallas_call(functools.partial(attend_forward_kernel, members), in_spec...  67.6 us
    reduce_scatter x1, waiting for transfers between devices, shards(): lax.psum_scatter(grad_ffn_inner.astype(jnp.bfloat16), 'shard', scatter_di...  49.8 us
    reduce_scatter x1, waiting for transfers between devices, shards(): lax.psum_scatter(grad_ffn_outer.astype(jnp.bfloat16), 'shard', scatter_di...  48.9 us
    psum x1, waiting for transfers between devices, shards(): lax.psum(shared[0].astype(jnp.bfloat16), 'ctx').astype(jnp.float32)  42 us
    dot_general x1, matrix products, shards(): jnp.einsum('stgi,gio->stgo', hidden_low, full_inner, preferred_element_ty...  33.3 us
    unnamed x234, local copies, waits for them, and re-layouts  31.4 us
    unnamed x2, blocking collectives  30.8 us
  transfers between devices with their start and end apart: 17, of which 9 were waited for; matrix products, arithmetic and copies ran while one was open for 19% of the time, Pallas kernels for 7%

profile of v1, /device:TPU:0, one launch (start us, length us, event | category | flops | bytes accessed | tf_op | source)
XLA Modules:
  0.0 907.5 jit_solution(13435835676812919637)
XLA Ops:
  18.8 13.5 %all-reduce.29 = (bf16[768]{0:T(1024)(128)(2,1)S(1)}, bf16[768]{0:T(1024)(128)(2,1)S(1)}, bf16[768]{0:T(1024)(128)(2,1)S(1)}) all-reduce(bf16[768]{0:T(1024)(128)(2,1)S(1)} %dynamic-update-slice.1, bf16[768]{0:T(1024)(128)(2,1)S(1)} %dynamic-update-slice, ...), channel_id=1, replica_groups=mesh['ctx'=8,'shard'=4] {'shard'}, use_global_device_ids=true, to_apply=%add.19 | all-reduce | flops 2304 | bytes 9216
  32.9 13.4 %all-gather = bf16[4,192,9]{1,2,0:T(8,128)(2,1)S(1)} all-gather(bf16[1,192,9]{1,2,0:T(8,128)(2,1)S(1)} %bitcast.318), channel_id=1, replica_groups=mesh['ctx'=8,'shard'=4] {'shard'}, dimensions={0}, use_global_device_ids=true | all-gather | bytes 17280 | tf_op jit(solution)/shard_map/all_gather | solution.py:474
  48.2 18.6 %all_gather.42 = bf16[768,384]{1,0:T(8,128)(2,1)} all-gather(bf16[192,384]{1,0:T(8,128)(2,1)S(1)} %copy-done.61), channel_id=1, replica_groups=mesh['ctx'=8,'shard'=4] {'shard'}, dimensions={0}, use_global_device_ids=true | all-gather | bytes 737280 | tf_op jit(solution)/shard_map/all_gather | solution.py:475
  66.8 22.5 %all_gather.44 = bf16[768,384]{1,0:T(8,128)(2,1)} all-gather(bf16[192,384]{1,0:T(8,128)(2,1)S(1)} %copy-done.62), channel_id=1, replica_groups=mesh['ctx'=8,'shard'=4] {'shard'}, dimensions={0}, use_global_device_ids=true | all-gather | bytes 737280 | tf_op jit(solution)/shard_map/all_gather | solution.py:477
  89.3 23.4 %all_gather.40 = bf16[384,768]{1,0:T(8,128)(2,1)} all-gather(bf16[96,768]{1,0:T(8,128)(2,1)} %param.22), channel_id=1, replica_groups=mesh['ctx'=8,'shard'=4] {'shard'}, dimensions={0}, use_global_device_ids=true | all-gather | bytes 737280 | tf_op jit(solution)/shard_map/all_gather | solution.py:478
  112.7 23.0 %all_gather.45 = bf16[384,768]{1,0:T(8,128)(2,1)} all-gather(bf16[96,768]{1,0:T(8,128)(2,1)} %param.23), channel_id=1, replica_groups=mesh['ctx'=8,'shard'=4] {'shard'}, dimensions={0}, use_global_device_ids=true | all-gather | bytes 737280 | tf_op jit(solution)/shard_map/all_gather | solution.py:479
  135.7 14.1 %all-gather.1 = bf16[4,96,54]{1,2,0:T(8,128)(2,1)S(1)} all-gather(bf16[1,96,54]{1,2,0:T(8,128)(2,1)} %bitcast.317), channel_id=1, replica_groups=mesh['ctx'=8,'shard'=4] {'shard'}, dimensions={0}, use_global_device_ids=true | all-gather | bytes 51840 | tf_op jit(solution)/shard_map/all_gather | solution.py:476
  151.3 4.7 fusion.36
  159.3 3.0 copy.215
  164.4 4.4 convolution_convert_fusion
  192.9 67.6 %shard_map.262 = (bf16[3,4,2,512,128]{4,3,2,1,0:T(8,128)(2,1)}, bf16[3,4,256,128]{3,2,1,0:T(8,128)(2,1)}, f32[3,4,256,128]{3,2,1,0:T(8,128)}, f32[3,4,2,2,8,128]{5,4,3,2,1,0:T(8,128)}, bf16[4,3,256,128]{3,2,1,0:T(8,128)(2,1)}) custom-call(bf16[4,3,512,128]{3,2,1,0:T(8,128)(2,1)} %copy.209.kv_in, bf16[4,3,256,128]{3,2,1,0:T(8,128)(2,1)} %copy.210.q_in), custom_call_target="tpu_custom_call" | custom-call | flops 6442450944 | bytes 8388608 | tf_op jit(solution)/shard_map/pallas_call | solution.py:221
  265.9 3.5 add_convert_fusion.2
  272.9 4.4 reshape.162
  277.3 4.9 copy.270
  282.2 33.3 %fusion.9 = (bf16[2,512,2,1536]{3,1,0,2:T(8,128)(2,1)}, f32[2,512,2,1536]{3,1,0,2:T(8,128)}, f32[2,2,512,1536]{3,2,1,0:T(8,128)}) fusion(bf16[2,512,2,384]{1,3,0,2:T(8,128)(2,1)} %copy.270, bf16[2,384,1536]{2,1,0:T(8,128)(2,1)} %all-gather.8.cloned.1.call-done), kind=kOutput, calls=%fused_computation.17 | convolution fusion | flops 2620391424 | bytes 35389440 | tf_op jit(solution)/shard_map/stgi,gio->stgo/dot_general | solution.py:545
  315.5 7.8 fusion.63
  323.3 5.8 copy.231
  329.1 5.5 reshape.163
  343.7 13.4 %fusion.6 = bf16[2,512,2,1536]{3,1,0,2:T(8,128)(2,1)} fusion(f32[2,512,2,1536]{3,1,0,2:T(8,128)} %get-tuple-element.153, f32[2,2,512,1536]{3,2,1,0:T(8,128)} %get-tuple-element.191, bf16[2,1536,384]{1,2,0:T(8,128)(2,1)S(1)} %copy-done.95, bf16[2,64,2,8,384]{4,3,2,1,0:T(8,128)(2,1)S(1)} %bitcast.300), kind=kOutput, calls=%fused_computation.9 | convolution fusion | flops 2459959296 | bytes 35389440 | tf_op jit(solution)/shard_map/stgi,goi->stgo/dot_general | solution.py:565
  357.1 7.1 fusion.60
  364.1 5.8 copy.234
  369.9 5.5 reshape.165
  375.5 5.2 multiply_reduce_fusion
  387.6 94.1 %shard_map.263 = (bf16[4,3,256,128]{3,2,1,0:T(8,128)(2,1)}, bf16[4,3,512,128]{3,2,1,0:T(8,128)(2,1)}) custom-call(bf16[4,3,256,128]{3,2,1,0:T(8,128)(2,1)} %copy.237.d_in, bf16[3,4,2,512,128]{4,3,2,1,0:T(8,128)(2,1)} %get-tuple-element.23.kv_all, bf16[3,4,256,128]{3,2,1,0:T(8,128)(2,1)} %get-tuple-element.24.q_all, ...), custom_call_target="tpu_custom_call" | custom-call | flops 16106127360 | bytes 8388608 | tf_op jit(solution)/shard_map/pallas_call | solution.py:407
  488.1 9.1 %multiply_reduce_fusion.5 = (f32[2,512,6]{1,2,0:T(8,128)S(1)}, f32[2,512,6]{1,2,0:T(8,128)S(1)}, f32[2,512,6]{1,2,0:T(8,128)S(1)}, f32[2,512,6]{1,2,0:T(8,128)S(...) fusion(f32[2,512,6,64]{1,3,2,0:T(8,128)} %bitcast.288, ...), kind=kLoop, calls=%fused_computation.142 | loop fusion | flops 10561536 | bytes 30326784 | tf_op jit(solution)/shard_map/reduce_sum | solution.py:594
  501.8 10.1 %pad_add_fusion.1 = f32[2,520,6,64]{1,3,2,0:T(8,128)} fusion(f32[2,512,6,64]{1,3,2,0:T(8,128)} %get-tuple-element.175, f32[2,512,6,64]{1,3,2,0:T(8,128)} %get-tuple-element.174, f32[2,512,6,64]{1,3,2,0:T(8,128)} %get-tuple-element.173, f32[2,512,6,64]{1,3,2,0:T(8,128)} %get-tuple-element.172, f32[2,512,6,64]{1,3,2,0:T(8,128)} %get-tuple-element.171, ...), kind=kLoop, calls=%fused_computation.118 | loop fusion | flops 3194880 | bytes 15753216 | tf_op jit(solution)/shard_map/add | solution.py:628
  513.9 13.2 %fusion.44 = (bf16[768]{0:T(1024)(128)(2,1)S(1)}, bf16[768]{0:T(1024)(128)(2,1)S(1)}, bf16[768]{0:T(1024)(128)(2,1)S(1)}, bf16[768]{0:T(1024)(128)(2,1)S(1)}, bf...) fusion(bf16[2,516,768]{2,1,0:T(8,128)(2,1)S(1)} %copy-done.6, ...), kind=kOutput, calls=%fused_computation.87 | convolution fusion | flops 639755520 | bytes 29729280 | tf_op jit(solution)/shard_map/sta,ia->sti/dot_general | solution.py:610
  530.2 5.8 pad_add_fusion
  540.2 3.2 collective-permute-done.3
  553.9 5.0 fusion.50
  558.9 4.0 copy.307
  564.8 3.2 fusion.87
  568.0 3.7 fusion.84
  571.8 8.2 bitcast_convert_fusion
  580.2 6.8 bitcast_convert_fusion.1
  593.6 16.7 %reduce-scatter.28.cloned.1.call-done = bf16[192,1152]{1,0:T(8,128)(2,1)} async-done(((bf16[768,1152]{1,0:T(8,128)(2,1)}), bf16[192,1152]{1,0:T(8,128)(2,1)}) %reduce-scatter.28.cloned.1.call-update) | async-done | bytes 442384
  612.5 21.3 %reduce-scatter.20.cloned.1.call-done = bf16[96,768]{1,0:T(8,128)(2,1)} async-done(((bf16[384,768]{1,0:T(8,128)(2,1)}), bf16[96,768]{1,0:T(8,128)(2,1)}) %reduce-scatter.20.cloned.1.call-update) | async-done | bytes 147472 | tf_op jit(solution)/shard_map/reduce_scatter | solution.py:684
  633.7 22.8 %reduce-scatter.22.cloned.1.call-done = bf16[96,768]{1,0:T(8,128)(2,1)} async-done(((bf16[384,768]{1,0:T(8,128)(2,1)}), bf16[96,768]{1,0:T(8,128)(2,1)}) %reduce-scatter.22.cloned.1.call-update) | async-done | bytes 147472 | tf_op jit(solution)/shard_map/reduce_scatter | solution.py:687
  656.5 23.3 %reduce-scatter.18.cloned.1.call-done = bf16[192,384]{1,0:T(8,128)(2,1)} async-done(((bf16[768,384]{1,0:T(8,128)(2,1)}), bf16[192,384]{1,0:T(8,128)(2,1)}) %reduce-scatter.18.cloned.1.call-update) | async-done | bytes 147472 | tf_op jit(solution)/shard_map/reduce_scatter | solution.py:675
  679.8 48.9 %reduce-scatter.26.cloned.1.call-done = bf16[2,384,384]{2,1,0:T(8,128)(2,1)} async-done(((bf16[2,1536,384]{2,1,0:T(8,128)(2,1)}), bf16[2,384,384]{2,1,0:T(8,128)(2,1)}) %reduce-scatter.26.cloned.1.call-update) | async-done | bytes 589840 | tf_op jit(solution)/shard_map/reduce_scatter | solution.py:699
  728.7 49.8 %reduce-scatter.24.cloned.1.call-done = bf16[2,96,1536]{2,1,0:T(8,128)(2,1)} async-done(((bf16[2,384,1536]{2,1,0:T(8,128)(2,1)}), bf16[2,96,1536]{2,1,0:T(8,128)(2,1)}) %reduce-scatter.24.cloned.1.call-update) | async-done | bytes 589840 | tf_op jit(solution)/shard_map/reduce_scatter | solution.py:696
  778.7 5.5 fusion.66
  784.1 17.3 %all-reduce.28 = (bf16[768]{0:T(1024)(128)(2,1)S(1)}, bf16[768]{0:T(1024)(128)(2,1)S(1)}, bf16[768]{0:T(1024)(128)(2,1)S(1)}, bf16[768]{0:T(1024)(128)(2,1)S(1)}, bf16[768]{0:T(1024)(128)(2,1)S(1)}) all-reduce(bf16[768]{0:T(1024)(128)(2,1)S(1)} %dynamic-update-slice.3, ...), channel_id=1, replica_groups=mesh['ctx'=8,'shard'=4] {'shard'}, use_global_device_ids=true, to_apply=%add.21 | all-reduce | flops 3840 | bytes 15360
  801.7 3.6 add_convert_fusion
  805.3 7.4 slice_add_fusion
  813.6 6.8 reduce-scatter.32.cloned.1.call-done
  821.2 22.8 %all-reduce.26 = (bf16[9,192]{1,0:T(8,128)(2,1)S(1)}, bf16[96,54]{0,1:T(8,128)(2,1)S(1)}, bf16[192]{0:T(256)(128)(2,1)S(1)}, bf16[192]{0:T(256)(128)(2,1)S(1)}, ...) all-reduce(bf16[9,192]{1,0:T(8,128)(2,1)S(1)} %copy.310, ...), channel_id=1, replica_groups=mesh['ctx'=8,'shard'=4] {'ctx'}, use_global_device_ids=true, to_apply=%region_32.0 | all-reduce | flops 7680 | bytes 30720 | tf_op jit(solution)/shard_map/psum | solution.py:711
  847.5 42.0 %all-reduce.32.cloned.1.call-done = (bf16[192,1152]{0,1:T(8,128)(2,1)}, bf16[192,384]{0,1:T(8,128)(2,1)}, bf16[192,384]{1,0:T(8,128)(2,1)}, bf16[96,768]{1,0:T(8...) async-done(((bf16[192,1152]{0,1:T(8,128)(2,1)}, bf16[192,384]{0,1:T(8,128)(2,1)}, bf16[192,384]{1,0:T(8,128)(2,1)}, ...) | async-done | bytes 2211856 | tf_op jit(solution)/shard_map/psum | solution.py:710
  (380 shorter events, 125.3 us)
Async XLA Ops:
  7.2 10.9 %copy-start.96 = (bf16[192]{0:T(256)(128)(2,1)S(1)}, bf16[192]{0:T(256)(128)(2,1)}, u32[]{:S(2)}) copy-start(bf16[192]{0:T(256)(128)(2,1)} %param.28) | copy-start | bytes 1156
  7.2 11.1 %copy-start.97 = (bf16[192]{0:T(256)(128)(2,1)S(1)}, bf16[192]{0:T(256)(128)(2,1)}, u32[]{:S(2)}) copy-start(bf16[192]{0:T(256)(128)(2,1)} %param.24) | copy-start | bytes 1156
  7.2 11.3 %copy-start.98 = (bf16[192]{0:T(256)(128)(2,1)S(1)}, bf16[192]{0:T(256)(128)(2,1)}, u32[]{:S(2)}) copy-start(bf16[192]{0:T(256)(128)(2,1)} %param.25) | copy-start | bytes 1156
  7.2 25.7 %copy-start.92 = (bf16[9,192]{1,0:T(8,128)(2,1)S(1)}, bf16[9,192]{1,0:T(8,128)(2,1)}, u32[]{:S(2)}) copy-start(bf16[9,192]{1,0:T(8,128)(2,1)} %param.18) | copy-start | bytes 10372
  7.2 40.9 %copy-start.61 = (bf16[192,384]{1,0:T(8,128)(2,1)S(1)}, bf16[192,384]{1,0:T(8,128)(2,1)}, u32[]{:S(2)}) copy-start(bf16[192,384]{1,0:T(8,128)(2,1)} %param.19) | copy-start | bytes 442372
  7.3 157.1 %all-gather.6.cloned.1.call-start = ((), (), s32[]{:S(2)}) async-start(), calls=%async_computation.9 | async-start | bytes 2211840 | tf_op jit(solution)/shard_map/all_gather | solution.py:473
  8.0 274.2 %all-gather.8.cloned.1.call-start = ((), (), s32[]{:S(2)}) async-start(), calls=%async_computation.10 | async-start | bytes 2949120 | tf_op jit(solution)/shard_map/all_gather | solution.py:482
  8.7 58.0 %copy-start.62 = (bf16[192,384]{1,0:T(8,128)(2,1)S(1)}, bf16[192,384]{1,0:T(8,128)(2,1)}, u32[]{:S(2)}) copy-start(bf16[192,384]{1,0:T(8,128)(2,1)} %param.21) | copy-start | bytes 442372
  8.8 306.8 %all-gather.10.cloned.1.call-start = ((), (), s32[]{:S(2)}) async-start(), calls=%async_computation.11 | async-start | bytes 2949120 | tf_op jit(solution)/shard_map/all_gather | solution.py:483
  10.2 141.1 %collective-permute-start = (bf16[2,4,768]{2,1,0:T(4,128)(2,1)}, bf16[2,4,768]{2,1,0:T(4,128)(2,1)}, u32[]{:S(2)}, u32[]{:S(2)}) collective-permute-start(bf16[2,4,768]{2,1,0:T(4,128)(2,1)} %get-tuple-element.176), channel_id=1, source_target_pairs={{0,4},{4,8},{8,12},{12,16},{16,20},{20,24},{24,28},{1,5},{5,9},{9,... | collective-permute-start | bytes 36872 | tf_op jit(solution)/shard_map/ppermute | solution.py:27
  13.1 137.4 %collective-permute-start.1 = (bf16[2,4,768]{2,1,0:T(4,128)(2,1)}, bf16[2,4,768]{2,1,0:T(4,128)(2,1)}, u32[]{:S(2)}, u32[]{:S(2)}) collective-permute-start(bf16[2,4,768]{2,1,0:T(4,128)(2,1)} %get-tuple-element.177), channel_id=1, source_target_pairs={{4,0},{8,4},{12,8},{16,12},{20,16},{24,20},{28,24},{5,1},{9,5},{13... | collective-permute-start | bytes 36872 | tf_op jit(solution)/shard_map/ppermute | solution.py:30
  16.6 575.3 %reduce-scatter.34.cloned.1.call-start = ((), (), s32[]{:S(2)}) async-start(), calls=%async_computation.20 | async-start | bytes 737280
  48.1 107.9 %copy-start.71 = (f32[768]{0:T(1024)}, f32[768]{0:T(1024)S(1)}, u32[]{:S(2)}) copy-start(f32[768]{0:T(1024)S(1)} %get-tuple-element.119) | copy-start | bytes 9220
  48.1 107.9 %copy-start.73 = (f32[768]{0:T(1024)}, f32[768]{0:T(1024)S(1)}, u32[]{:S(2)}) copy-start(f32[768]{0:T(1024)S(1)} %get-tuple-element.125) | copy-start | bytes 9220
  48.1 107.9 %copy-start.75 = (f32[768]{0:T(1024)}, f32[768]{0:T(1024)S(1)}, u32[]{:S(2)}) copy-start(f32[768]{0:T(1024)S(1)} %get-tuple-element.126) | copy-start | bytes 9220
  48.2 107.9 %copy-start.77 = (f32[768]{0:T(1024)}, f32[768]{0:T(1024)S(1)}, u32[]{:S(2)}) copy-start(f32[768]{0:T(1024)S(1)} %get-tuple-element.127) | copy-start | bytes 9220
  48.2 107.9 %copy-start.79 = (f32[768]{0:T(1024)}, f32[768]{0:T(1024)S(1)}, u32[]{:S(2)}) copy-start(f32[768]{0:T(1024)S(1)} %get-tuple-element.120) | copy-start | bytes 9220
  48.2 107.9 %copy-start.81 = (f32[768]{0:T(1024)}, f32[768]{0:T(1024)S(1)}, u32[]{:S(2)}) copy-start(f32[768]{0:T(1024)S(1)} %get-tuple-element.121) | copy-start | bytes 9220
  48.2 107.9 %copy-start.83 = (f32[768]{0:T(1024)}, f32[768]{0:T(1024)S(1)}, u32[]{:S(2)}) copy-start(f32[768]{0:T(1024)S(1)} %get-tuple-element.122) | copy-start | bytes 9220
  48.2 107.9 %copy-start.85 = (f32[768]{0:T(1024)}, f32[768]{0:T(1024)S(1)}, u32[]{:S(2)}) copy-start(f32[768]{0:T(1024)S(1)} %get-tuple-element.123) | copy-start | bytes 9220
  48.2 107.9 %copy-start.87 = (f32[768]{0:T(1024)}, f32[768]{0:T(1024)S(1)}, u32[]{:S(2)}) copy-start(f32[768]{0:T(1024)S(1)} %get-tuple-element.124) | copy-start | bytes 9220
  164.4 101.4 %copy-start = (f32[2,520,384]{1,2,0:T(8,128)}, f32[2,520,384]{1,2,0:T(8,128)S(1)}, u32[]{:S(2)}) copy-start(f32[2,520,384]{1,2,0:T(8,128)S(1)} %fusion.69) | copy-start | bytes 4792324
  270.7 109.9 %copy-start.2 = (f32[2,512,768]{2,1,0:T(8,128)}, f32[2,512,768]{2,1,0:T(8,128)S(1)}, u32[]{:S(2)}) copy-start(f32[2,512,768]{2,1,0:T(8,128)S(1)} %get-tuple-element.190) | copy-start | bytes 9437188
  339.9 35.5 %copy-start.65 = (f32[2,512]{1,0:T(2,128)}, f32[2,512]{1,0:T(2,128)S(1)}, u32[]{:S(2)}) copy-start(f32[2,512]{1,0:T(2,128)S(1)} %add_rsqrt_fusion) | copy-start | bytes 12292
  343.1 14.0 %copy-start.39 = (bf16[2,512,768]{2,1,0:T(8,128)(2,1)}, bf16[2,512,768]{2,1,0:T(8,128)(2,1)S(1)}, u32[]{:S(2)}) copy-start(bf16[2,512,768]{2,1,0:T(8,128)(2,1)S(1)} %fusion.91) | copy-start | bytes 4718596
  343.7 13.4 %copy-start.94 = (bf16[2,384,1536]{2,1,0:T(8,128)(2,1)S(1)}, bf16[2,384,1536]{2,1,0:T(8,128)(2,1)}, u32[]{:S(2)}) copy-start(bf16[2,384,1536]{2,1,0:T(8,128)(2,1)} %all-gather.8.cloned.1.call-done) | copy-start | bytes 7077892
  513.9 13.3 %copy-start.72 = (f32[768]{0:T(1024)S(1)}, f32[768]{0:T(1024)}, u32[]{:S(2)}) copy-start(f32[768]{0:T(1024)} %copy-done.71) | copy-start | bytes 9220
  513.9 13.3 %copy-start.74 = (f32[768]{0:T(1024)S(1)}, f32[768]{0:T(1024)}, u32[]{:S(2)}) copy-start(f32[768]{0:T(1024)} %copy-done.73) | copy-start | bytes 9220
  513.9 13.3 %copy-start.76 = (f32[768]{0:T(1024)S(1)}, f32[768]{0:T(1024)}, u32[]{:S(2)}) copy-start(f32[768]{0:T(1024)} %copy-done.75) | copy-start | bytes 9220
  513.9 13.3 %copy-start.78 = (f32[768]{0:T(1024)S(1)}, f32[768]{0:T(1024)}, u32[]{:S(2)}) copy-start(f32[768]{0:T(1024)} %copy-done.77) | copy-start | bytes 9220
  536.3 3.8 collective-permute-start.2
  538.3 5.0 collective-permute-start.3
  547.8 62.6 %reduce-scatter.28.cloned.1.call-start = ((), (), s32[]{:S(2)}) async-start(), calls=%async_computation.17 | async-start | bytes 2211840
  563.0 70.7 %reduce-scatter.20.cloned.1.call-start = ((), (), s32[]{:S(2)}) async-start(), calls=%async_computation.13 | async-start | bytes 737280 | tf_op jit(solution)/shard_map/reduce_scatter | solution.py:684
  564.7 91.8 %reduce-scatter.22.cloned.1.call-start = ((), (), s32[]{:S(2)}) async-start(), calls=%async_computation.14 | async-start | bytes 737280 | tf_op jit(solution)/shard_map/reduce_scatter | solution.py:687
  567.9 111.9 %reduce-scatter.18.cloned.1.call-start = ((), (), s32[]{:S(2)}) async-start(), calls=%async_computation.12 | async-start | bytes 737280 | tf_op jit(solution)/shard_map/reduce_scatter | solution.py:675
  571.8 157.0 %reduce-scatter.26.cloned.1.call-start = ((), (), s32[]{:S(2)}) async-start(), calls=%async_computation.16 | async-start | bytes 2949120 | tf_op jit(solution)/shard_map/reduce_scatter | solution.py:699
  580.1 198.5 %reduce-scatter.24.cloned.1.call-start = ((), (), s32[]{:S(2)}) async-start(), calls=%async_computation.15 | async-start | bytes 2949120 | tf_op jit(solution)/shard_map/reduce_scatter | solution.py:696
  587.0 225.8 %reduce-scatter.30.cloned.1.call-start = ((), (), s32[]{:S(2)}) async-start(), calls=%async_computation.18 | async-start | bytes 245760
  588.3 232.1 %reduce-scatter.32.cloned.1.call-start = ((), (), s32[]{:S(2)}) async-start(), calls=%async_computation.19 | async-start | bytes 122880
  589.8 188.8 %copy-start.38 = (bf16[2,512,768]{2,1,0:T(8,128)(2,1)S(1)}, bf16[2,512,768]{2,1,0:T(8,128)(2,1)}, u32[]{:S(2)}) copy-start(bf16[2,512,768]{2,1,0:T(8,128)(2,1)} %copy.264) | copy-start | bytes 4718596
  590.6 298.9 %all-reduce.32.cloned.1.call-start = ((), (), s32[]{:S(2)}) async-start(), calls=%async_computation.21 | async-start | bytes 4816896 | tf_op jit(solution)/shard_map/psum | solution.py:710
  590.9 187.7 %copy-start.43 = (bf16[2,512,384]{2,1,0:T(8,128)(2,1)S(1)}, bf16[2,512,384]{2,1,0:T(8,128)(2,1)}, u32[]{:S(2)}) copy-start(bf16[2,512,384]{2,1,0:T(8,128)(2,1)} %copy-done.42) | copy-start | bytes 2359300
  778.6 23.1 %copy-start.64 = (f32[768]{0:T(1024)S(1)}, f32[768]{0:T(1024)}, u32[]{:S(2)}) copy-start(f32[768]{0:T(1024)} %convert_element_type.282) | copy-start | bytes 9220
  778.6 23.1 %copy-start.66 = (f32[2,512]{1,0:T(2,128)S(1)}, f32[2,512]{1,0:T(2,128)}, u32[]{:S(2)}) copy-start(f32[2,512]{1,0:T(2,128)} %copy-done.65) | copy-start | bytes 12292
  784.1 21.2 %copy-start.3 = (f32[2,512,768]{2,1,0:T(8,128)S(1)}, f32[2,512,768]{2,1,0:T(8,128)}, u32[]{:S(2)}) copy-start(f32[2,512,768]{2,1,0:T(8,128)} %copy-done.2) | copy-start | bytes 9437188
  784.1 21.2 %copy-start.68 = (f32[2,512]{1,0:T(2,128)S(1)}, f32[2,512]{1,0:T(2,128)}, u32[]{:S(2)}) copy-start(f32[2,512]{1,0:T(2,128)} %copy-done.67) | copy-start | bytes 12292
  784.1 21.2 %copy-start.70 = (f32[2,512]{1,0:T(2,128)S(1)}, f32[2,512]{1,0:T(2,128)}, u32[]{:S(2)}) copy-start(f32[2,512]{1,0:T(2,128)} %copy-done.69) | copy-start | bytes 12292
  (70 other events, 291.7 us)
Sparse Core Ops, SparseCore 0:
  9.7 48.0 all-gather.5
  59.3 74.0 all-gather.7
  135.0 49.6 all-gather.9
  547.9 23.3 reduce-scatter.33
  573.5 36.8 reduce-scatter.27
  612.6 21.0 reduce-scatter.19
  636.1 20.3 reduce-scatter.21
  659.4 20.3 reduce-scatter.17
  682.2 46.4 reduce-scatter.25
  731.0 47.5 reduce-scatter.23
  781.5 18.9 reduce-scatter.29
  803.2 17.2 reduce-scatter.31
  825.8 63.7 all-reduce.31

commit v2 on v1

--- a/solution.py
+++ b/solution.py
@@ -92,23 +92,324 @@
     pl.semaphore_wait(barrier, len(peers))
 
 
-def attend_forward_kernel(
-    members, kv_in, q_in, kv_all, q_all, out_all, lse, ctx_out,
-    out_send, kv_s, kv_r, q_s, q_r, f_s, f_r, o_s, o_r, local,
-):
+class Place:
+    def __init__(self, members, shards):
+        self.members, self.shards = members, shards
+        self.me = lax.axis_index("ctx")
+        self.z = lax.axis_index("shard")
+        self.quad, self.sub = self.me // members, self.me % members
+
+    def peer(self, step):
+        return ((self.quad + step) % QUADS * self.members + self.sub, self.z)
+
+    def sibling(self, step):
+        return (self.quad * self.members + (self.sub + step) % self.members, self.z)
+
+    def behind(self, step):
+        return (self.quad + QUADS - step) % QUADS
+
+    def along(self, step):
+        return (self.me, (self.z + step) % self.shards)
+
+    def z_behind(self, step):
+        return (self.z + self.shards - step) % self.shards
+
+    def greet(self, with_shard):
+        peers = [self.peer(k) for k in range(1, QUADS)]
+        peers += [self.sibling(m) for m in range(1, self.members)]
+        if with_shard:
+            peers += [self.along(d) for d in range(1, self.shards)]
+        greet(peers)
+
+
+class Pieces:
+    def __init__(self, place, rows, columns, col_split):
+        count = QUADS * place.members
+        self.place, self.rows, self.col_split = place, rows, col_split
+        self.piece_rows = rows // (count // col_split)
+        self.piece_cols = columns // col_split
+
+    def at(self, ref, z, quad, sub):
+        index = quad * self.place.members + sub
+        top = pl.multiple_of(z * self.rows + index // self.col_split * self.piece_rows, 16)
+        left = pl.multiple_of(index % self.col_split * self.piece_cols, 128)
+        return ref.at[pl.ds(top, self.piece_rows), pl.ds(left, self.piece_cols)]
+
+
+def fits(rows, columns, members, col_split):
+    count = QUADS * members
+    if count % col_split:
+        return False
+    row_split = count // col_split
+    return rows % (16 * row_split) == 0 and columns % (128 * col_split) == 0
+
+
+class Gather:
+    def __init__(self, place, shard_ref, full_ref, col_split, sems):
+        self.place, self.shard_ref, self.full_ref = place, shard_ref, full_ref
+        rows, columns = shard_ref.shape
+        self.rows = rows
+        self.pieces = Pieces(place, rows, columns, col_split)
+        self.z_s, self.z_r, self.q_s, self.q_r, self.f_s, self.f_r, self.local = sems
+
+    @staticmethod
+    def semaphores(members, shards):
+        dma = pltpu.SemaphoreType.DMA
+        return [
+            dma((shards,)), dma((shards,)), dma((shards, QUADS)), dma((shards, QUADS)),
+            dma((shards, QUADS, members)), dma((shards, QUADS, members)), dma((1,)),
+        ]
+
+    def z_copy(self, d):
+        p = self.place
+        return remote(
+            self.pieces.at(self.shard_ref, 0, p.quad, p.sub), self.pieces.at(self.full_ref, p.z, p.quad, p.sub),
+            self.z_s.at[d], self.z_r.at[d], p.along(d),
+        )
+
+    def q_copy(self, d, k):
+        p = self.place
+        block = self.pieces.at(self.full_ref, p.z_behind(d), p.quad, p.sub)
+        return remote(block, block, self.q_s.at[d, k], self.q_r.at[d, k], p.peer(k))
+
+    def f_copy(self, d, k, m):
+        p = self.place
+        block = self.pieces.at(self.full_ref, p.z_behind(d), p.behind(k), p.sub)
+        return remote(block, block, self.f_s.at[d, k, m], self.f_r.at[d, k, m], p.sibling(m))
+
+    def own_copy(self):
+        top = pl.multiple_of(self.place.z * self.rows, 16)
+        return pltpu.make_async_copy(
+            self.shard_ref, self.full_ref.at[pl.ds(top, self.rows), :], self.local.at[0]
+        )
+
+    def start(self):
+        for d in range(1, self.place.shards):
+            self.z_copy(d).start()
+        self.own_copy().start()
+
+    def relay(self):
+        for d in range(1, self.place.shards):
+            self.z_copy(d).wait_recv()
+            for k in range(1, QUADS):
+                self.q_copy(d, k).start()
+            for m in range(1, self.place.members):
+                self.f_copy(d, 0, m).start()
+
+    def share(self):
+        for d in range(1, self.place.shards):
+            for k in range(1, QUADS):
+                self.q_copy(d, k).wait_recv()
+                for m in range(1, self.place.members):
+                    self.f_copy(d, k, m).start()
+
+    def end(self):
+        for d in range(1, self.place.shards):
+            self.z_copy(d).wait_send()
+            for k in range(QUADS):
+                if k:
+                    self.q_copy(d, k).wait_send()
+                for m in range(1, self.place.members):
+                    self.f_copy(d, k, m).wait()
+        self.own_copy().wait()
+
+
+class Reduce:
+    def __init__(self, place, part_ref, out_ref, col_split, scratch):
+        self.place, self.part_ref, self.out_ref = place, part_ref, out_ref
+        self.piece_rows, self.piece_cols = part_ref.shape[3:]
+        rows, columns = out_ref.shape
+        self.pieces = Pieces(place, rows, columns, col_split)
+        (
+            self.half, self.half_in, self.quad_in, self.block, self.z_in, self.last,
+            self.h_s, self.h_r, self.q_s, self.q_r, self.z_s, self.z_r, self.a_s, self.a_r, self.f_s, self.f_r, self.local,
+        ) = scratch
+
+    @staticmethod
+    def scratch(members, shards, rows, columns):
+        dma = pltpu.SemaphoreType.DMA
+        return [
+            pltpu.VMEM((shards, QUADS, rows, columns), BF),
+            pltpu.VMEM((members, shards, QUADS, rows, columns), BF),
+            pltpu.VMEM((QUADS, shards, rows, columns), BF),
+            pltpu.VMEM((shards, rows, columns), BF),
+            pltpu.VMEM((shards, rows, columns), BF),
+            pltpu.VMEM((rows, columns), BF),
+            dma((members,)), dma((members,)), dma((QUADS,)), dma((QUADS,)), dma((shards,)), dma((shards,)),
+            dma((QUADS,)), dma((QUADS,)), dma((QUADS, members)), dma((QUADS, members)), dma((1,)),
+        ]
+
+    def h_copy(self, m):
+        p = self.place
+        return remote(
+            self.part_ref.at[(p.sub + m) % p.members], self.half_in.at[m], self.h_s.at[m], self.h_r.at[m], p.sibling(m)
+        )
+
+    def q_copy(self, k):
+        p = self.place
+        return remote(
+            self.half.at[:, (p.quad + k) % QUADS], self.quad_in.at[k], self.q_s.at[k], self.q_r.at[k], p.peer(k)
+        )
+
+    def z_copy(self, d):
+        p = self.place
+        return remote(
+            self.block.at[(p.z + d) % p.shards], self.z_in.at[d], self.z_s.at[d], self.z_r.at[d], p.along(d)
+        )
+
+    def a_copy(self, k):
+        p = self.place
+        return remote(
+            self.last, self.pieces.at(self.out_ref, 0, p.quad, p.sub), self.a_s.at[k], self.a_r.at[k], p.peer(k)
+        )
+
+    def f_copy(self, k, m):
+        p = self.place
+        block = self.pieces.at(self.out_ref, 0, p.behind(k), p.sub)
+        return remote(block, block, self.f_s.at[k, m], self.f_r.at[k, m], p.sibling(m))
+
+    def own_copy(self):
+        p = self.place
+        return pltpu.make_async_copy(
+            self.last, self.pieces.at(self.out_ref, 0, p.quad, p.sub), self.local.at[0]
+        )
+
+    def start(self):
+        for m in range(1, self.place.members):
+            self.h_copy(m).start()
+
+    def to_quads(self):
+        for m in range(1, self.place.members):
+            self.h_copy(m).wait_recv()
+
+        def turn(i, carry):
+            z, q = i // QUADS, i % QUADS
+            total = self.part_ref[self.place.sub, z, q].astype(F32)
+            for m in range(1, self.place.members):
+                total = total + self.half_in[m, z, q].astype(F32)
+            self.half[z, q] = total.astype(BF)
+            return carry
+
+        lax.fori_loop(0, self.place.shards * QUADS, turn, 0)
+        for k in range(1, QUADS):
+            self.q_copy(k).start()
+
+    def to_shards(self):
+        for k in range(1, QUADS):
+            self.q_copy(k).wait_recv()
+
+        def turn(z, carry):
+            total = self.half[z, self.place.quad].astype(F32)
+            for k in range(1, QUADS):
+                total = total + self.quad_in[k, z].astype(F32)
+            self.block[z] = total.astype(BF)
+            return carry
+
+        lax.fori_loop(0, self.place.shards, turn, 0)
+        for d in range(1, self.place.shards):
+            self.z_copy(d).start()
+
+    def give(self):
+        total = self.block[self.place.z].astype(F32)
+        for d in range(1, self.place.shards):
+            self.z_copy(d).wait_recv()
+            total = total + self.z_in[d].astype(F32)
+        self.last[...] = total.astype(BF)
+        for k in range(1, QUADS):
+            self.a_copy(k).start()
+        self.own_copy().start()
+        self.own_copy().wait()
+        for m in range(1, self.place.members):
+            self.f_copy(0, m).start()
+
+    def share(self):
+        for k in range(1, QUADS):
+            self.a_copy(k).wait_recv()
+            for m in range(1, self.place.members):
+                self.f_copy(k, m).start()
+
+    def end(self):
+        for m in range(1, self.place.members):
+            self.h_copy(m).wait_send()
+        for k in range(1, QUADS):
+            self.q_copy(k).wait_send()
+            self.a_copy(k).wait_send()
+        for d in range(1, self.place.shards):
+            self.z_copy(d).wait_send()
+        for k in range(QUADS):
+            for m in range(1, self.place.members):
+                self.f_copy(k, m).wait()
+
+
+def cut(part, members, shards, col_split):
+    count = QUADS * members
+    row_split = count // col_split
+    piece_rows = part.shape[0] // (shards * row_split)
+    piece_cols = part.shape[1] // col_split
+    split = part.astype(BF).reshape(shards, row_split, piece_rows, col_split, piece_cols)
+    split = split.transpose(0, 1, 3, 2, 4).reshape(shards, QUADS, members, piece_rows, piece_cols)
+    return split.transpose(2, 0, 1, 3, 4)
+
+
+def gather_kernel(members, shards, split, shard_ref, full_ref, *sems):
+    place = Place(members, shards)
+    place.greet(True)
+    one = Gather(place, shard_ref, full_ref, split, sems)
+    one.start()
+    one.relay()
+    one.share()
+    one.end()
+
+
+def gather_weight(block, members, shards, split, number):
+    anywhere = pl.BlockSpec(memory_space=pl.ANY)
+    return pl.pallas_call(
+        functools.partial(gather_kernel, members, shards, split),
+        in_specs=[anywhere],
+        out_specs=anywhere,
+        out_shape=jax.ShapeDtypeStruct((shards * block.shape[0], block.shape[1]), BF),
+        scratch_shapes=Gather.semaphores(members, shards),
+        compiler_params=pltpu.CompilerParams(collective_id=number, has_side_effects=True),
+    )(block)
+
+
+def reduce_kernel(members, shards, split, part_ref, out_ref, *scratch):
+    place = Place(members, shards)
+    place.greet(True)
+    one = Reduce(place, part_ref, out_ref, split, scratch)
+    one.start()
+    one.to_quads()
+    one.to_shards()
+    one.give()
+    one.share()
+    one.end()
+
+
+def reduce_weight(part, members, shards, split, number):
+    pieces = cut(part, members, shards, split)
+    rows = part.shape[0] // shards
+    return pl.pallas_call(
+        functools.partial(reduce_kernel, members, shards, split),
+        in_specs=[pl.BlockSpec(memory_space=pltpu.VMEM)],
+        out_specs=pl.BlockSpec(memory_space=pl.ANY),
+        out_shape=jax.ShapeDtypeStruct((rows, part.shape[1]), BF),
+        scratch_shapes=Reduce.scratch(members, shards, *pieces.shape[3:]),
+        compiler_params=pltpu.CompilerParams(
+            collective_id=number, has_side_effects=True, vmem_limit_bytes=56 * 2**20
+        ),
+    )(pieces)
+
+
+def attend_forward_kernel(members, shards, splits, *refs):
+    count = len(splits)
+    kv_in, q_in, *blocks = refs[: 2 + count]
+    kv_all, q_all, out_all, lse, ctx_out, *fulls = refs[2 + count : 7 + 2 * count]
+    out_send, kv_s, kv_r, q_s, q_r, f_s, f_r, o_s, o_r, local, *sems = refs[7 + 2 * count :]
     rows = kv_in.shape[2]
     half = rows // 2
-    me = lax.axis_index("ctx")
-    shard = lax.axis_index("shard")
-    quad, sub = me // members, me % members
-
-    def peer(step):
-        return ((quad + step) % QUADS * members + sub, shard)
-
-    def sibling(step):
-        return (quad * members + (sub + step) % members, shard)
-
-    greet([peer(k) for k in range(1, QUADS)] + [sibling(m) for m in range(1, members)])
+    place = Place(members, shards)
+    quad, sub, peer, sibling = place.quad, place.sub, place.peer, place.sibling
+    place.greet(bool(splits))
 
     def kv_copy(h, k):
         return remote(
@@ -134,6 +435,12 @@
     own_q = pltpu.make_async_copy(q_in.at[quad], q_all.at[:, quad], local.at[1])
     own_kv.start()
     own_q.start()
+    gathers = [
+        Gather(place, block, full, split, sems[7 * j : 7 * j + 7])
+        for j, (block, full, split) in enumerate(zip(blocks, fulls, splits))
+    ]
+    for gather in gathers:
+        gather.start()
     for h in range(TRIPLE):
         for k in range(1, QUADS):
             kv_copy(h, k).start()
@@ -199,9 +506,23 @@
         def _():
             receive(h + 1)
 
+        if gathers:
+
+            @pl.when(step == 4)
+            def _():
+                for gather in gathers:
+                    gather.relay()
+
+            @pl.when(step == TRIPLE * QUADS - 1)
+            def _():
+                for gather in gathers:
+                    gather.share()
+
         return carry
 
     lax.fori_loop(0, TRIPLE * QUADS, block, 0)
+    for gather in gathers:
+        gather.end()
     for h in range(TRIPLE):
         for k in range(1, QUADS):
             out_copy(h, k - 1, k).wait()
@@ -211,7 +532,7 @@
             forward_copy(h, m).wait_send()
 
 
-def attend_forward(kv, q, members):
+def attend_forward(kv, q, members, shards, blocks, splits):
     rows = kv.shape[2]
     half = rows // 2
     vm = pl.BlockSpec(memory_space=pltpu.VMEM)
@@ -219,48 +540,49 @@
     dma = pltpu.SemaphoreType.DMA
     total = TRIPLE * QUADS * rows * QUADS * members * rows
     return pl.pallas_call(
-        functools.partial(attend_forward_kernel, members),
-        in_specs=[anywhere, anywhere],
-        out_specs=[vm, vm, vm, vm, anywhere],
+        functools.partial(attend_forward_kernel, members, shards, splits),
+        in_specs=[anywhere, anywhere] + [anywhere] * len(blocks),
+        out_specs=[vm, vm, vm, vm, anywhere] + [anywhere] * len(blocks),
         out_shape=[
             jax.ShapeDtypeStruct((TRIPLE, QUADS, members, rows, 2 * HEAD), BF),
             jax.ShapeDtypeStruct((TRIPLE, QUADS, half, 2 * HEAD), BF),
             jax.ShapeDtypeStruct((TRIPLE, QUADS, half, 2 * HEAD), F32),
             jax.ShapeDtypeStruct((TRIPLE, QUADS, 2, half // CHUNK, 8, CHUNK), F32),
             jax.ShapeDtypeStruct((QUADS, TRIPLE, half, 2 * HEAD), BF),
-        ],
+        ]
+        + [jax.ShapeDtypeStruct((shards * block.shape[0], block.shape[1]), BF) for block in blocks],
         scratch_shapes=[
             pltpu.VMEM((TRIPLE, QUADS, half, 2 * HEAD), BF),
             dma((TRIPLE, QUADS)), dma((TRIPLE, QUADS)), dma((TRIPLE, QUADS)), dma((TRIPLE, QUADS)),
             dma((TRIPLE, members)), dma((TRIPLE, members)), dma((TRIPLE, QUADS)), dma((TRIPLE, QUADS)),
             dma((2,)),
-        ],
+        ]
+        + Gather.semaphores(members, shards) * len(blocks),
         compiler_params=pltpu.CompilerParams(
             collective_id=1, has_side_effects=True, vmem_limit_bytes=56 * 2**20
         ),
         cost_estimate=pl.CostEstimate(flops=total * 256, bytes_accessed=8 * 2**20, transcendentals=total),
-    )(kv, q)
-
-
-def attend_backward_kernel(
-    members, d_in, kv_all, q_all, out_all, lse, dq_out, dkv_out,
-    d_all, q_zero, d_zero, stat, delta, dq_sum, dkv_sum, own_part, sib_send, sib_recv, dkv_send, dq_send,
-    d_s, d_r, p_s, p_r, k_s, k_r, g_s, g_r, local,
-):
+    )(kv, q, *blocks)
+
+
+def attend_backward_kernel(members, shards, splits, *refs):
+    count = len(splits)
+    d_in, kv_all, q_all, out_all, lse, *parts = refs[: 5 + count]
+    dq_out, dkv_out, *sums = refs[5 + count : 7 + 2 * count]
+    (
+        d_all, q_zero, d_zero, stat, delta, dq_sum, dkv_sum, own_part, sib_send, sib_recv, dkv_send, dq_send,
+        d_s, d_r, p_s, p_r, k_s, k_r, g_s, g_r, local, *scratch,
+    ) = refs[7 + 2 * count :]
     rows = kv_all.shape[3]
     half = rows // 2
-    me = lax.axis_index("ctx")
-    shard = lax.axis_index("shard")
-    quad, sub = me // members, me % members
     steps = TRIPLE * QUADS
-
-    def peer(step):
-        return ((quad + step) % QUADS * members + sub, shard)
-
-    def sibling(step):
-        return (quad * members + (sub + step) % members, shard)
-
-    greet([peer(k) for k in range(1, QUADS)] + [sibling(m) for m in range(1, members)])
+    place = Place(members, shards)
+    quad, sub, peer, sibling = place.quad, place.sub, place.peer, place.sibling
+    place.greet(bool(splits))
+    reduces = [
+        Reduce(place, one, total, split, scratch[17 * j : 17 * j + 17])
+        for j, (one, total, split) in enumerate(zip(parts, sums, splits))
+    ]
 
     def d_copy(h, k):
         return remote(
@@ -287,6 +609,8 @@
     for h in range(TRIPLE):
         for k in range(1, QUADS):
             d_copy(h, k).start()
+    for one in reduces:
+        one.start()
     own.wait()
     is_low = low_lanes()
 
@@ -382,6 +706,13 @@
             mine.start()
             mine.wait()
 
+        for j, one in enumerate(reduces):
+            for at, stage in ((j, one.to_quads), (j + 4, one.to_shards), (j + 6, one.give), (j + 8, one.share)):
+
+                @pl.when(step == at)
+                def _(stage=stage):
+                    stage()
+
         return carry
 
     lax.fori_loop(0, steps, block, 0)
@@ -394,9 +725,11 @@
             d_copy(h, k).wait_send()
             dkv_copy(h, k - 1, k).wait()
             dq_copy(h, k).wait()
-
-
-def attend_backward(d_context, kv_all, q_all, out_all, lse, members):
+    for one in reduces:
+        one.end()
+
+
+def attend_backward(d_context, kv_all, q_all, out_all, lse, members, shards, parts, splits):
     rows = kv_all.shape[3]
     half = rows // 2
     steps = TRIPLE * QUADS
@@ -405,13 +738,14 @@
     dma = pltpu.SemaphoreType.DMA
     total = TRIPLE * QUADS * rows * QUADS * members * rows
     return pl.pallas_call(
-        functools.partial(attend_backward_kernel, members),
-        in_specs=[anywhere, vm, vm, vm, vm],
-        out_specs=[anywhere, anywhere],
+        functools.partial(attend_backward_kernel, members, shards, splits),
+        in_specs=[anywhere, vm, vm, vm, vm] + [vm] * len(parts),
+        out_specs=[anywhere, anywhere] + [anywhere] * len(parts),
         out_shape=[
             jax.ShapeDtypeStruct((QUADS, TRIPLE, half, 2 * HEAD), BF),
             jax.ShapeDtypeStruct((QUADS, TRIPLE, rows, 2 * HEAD), BF),
-        ],
+        ]
+        + [jax.ShapeDtypeStruct(shape, BF) for _, shape in parts],
         scratch_shapes=[
             pltpu.VMEM((TRIPLE, QUADS, half, 2 * HEAD), BF),
             pltpu.VMEM((QUADS, rows, 2 * HEAD), BF),
@@ -429,12 +763,13 @@
             dma((steps, members)), dma((steps, members)),
             dma((TRIPLE, QUADS)), dma((TRIPLE, QUADS)), dma((TRIPLE, QUADS)), dma((TRIPLE, QUADS)),
             dma((2,)),
-        ],
+        ]
+        + sum((Reduce.scratch(members, shards, *one.shape[3:]) for one, _ in parts), []),
         compiler_params=pltpu.CompilerParams(
             collective_id=2, has_side_effects=True, vmem_limit_bytes=56 * 2**20
         ),
         cost_estimate=pl.CostEstimate(flops=total * 640, bytes_accessed=8 * 2**20, transcendentals=total),
-    )(d_context, kv_all, q_all, out_all, lse)
+    )(d_context, kv_all, q_all, out_all, lse, *[one for one, _ in parts])
 
 
 def pack_heads(values):
@@ -447,6 +782,9 @@
     half = packed.shape[2]
     split = packed.reshape(seqs, HEADS, half, 2, HEAD)
     return split.transpose(0, 3, 2, 1, 4).reshape(seqs, 2 * half, HEADS * HEAD)
+
+
+SPLITS = (2, 4, 1)
 
 
 def shards(
@@ -469,44 +807,54 @@
     attn_width = HEADS * HEAD
     half_kernel = KERNEL // 2
     seq_count, local_rows, model_width = hidden_in.shape
-    gathered = (
-        lax.all_gather(qkv_weight, "shard", axis=0, tiled=True),
-        lax.all_gather(conv_depth, "shard", axis=1, tiled=True),
-        lax.all_gather(conv_point, "shard", axis=0, tiled=True),
-        lax.all_gather(span_weight, "shard", axis=0, tiled=True),
-        lax.all_gather(conv_value, "shard", axis=0, tiled=True),
-        lax.all_gather(dense_attn, "shard", axis=0, tiled=True),
-        lax.all_gather(dense_conv, "shard", axis=0, tiled=True),
-        lax.all_gather(attn_norm_gain, "shard", axis=0, tiled=True),
-        lax.all_gather(attn_norm_bias, "shard", axis=0, tiled=True),
-        lax.all_gather(ffn_inner, "shard", axis=1, tiled=True),
-        lax.all_gather(ffn_outer, "shard", axis=1, tiled=True),
-        lax.all_gather(out_norm_gain, "shard", axis=0, tiled=True),
-        lax.all_gather(out_norm_bias, "shard", axis=0, tiled=True),
-    )
-    (
-        full_qkv,
-        full_depth,
-        full_point,
-        full_span,
-        full_value,
-        full_dense_attn,
-        full_dense_conv,
-        attn_gain_full,
-        attn_bias_full,
-        full_inner,
-        full_outer,
-        out_gain_full,
-        out_bias_full,
-    ) = gathered
+    members = lax.axis_size("ctx") // QUADS
+    shard_count = lax.axis_size("shard")
+    width_rows = model_width // shard_count
+    head_rows = attn_width // shard_count
+    small = jnp.concatenate(
+        [
+            jnp.pad(span_weight, ((0, width_rows - head_rows), (0, 64 - HEADS * KERNEL))),
+            conv_depth.T,
+            jnp.stack([attn_norm_gain, attn_norm_bias, out_norm_gain, out_norm_bias], axis=1),
+            jnp.zeros((width_rows, 128 - 64 - KERNEL - 4), jnp.bfloat16),
+        ],
+        axis=1,
+    )
+    first_block = jnp.concatenate([qkv_weight, conv_value, conv_point, small], axis=1)
+    second_block = jnp.concatenate([dense_attn, dense_conv, ffn_inner[0], ffn_inner[1]], axis=1)
+    third_block = jnp.concatenate([ffn_outer[0], ffn_outer[1]], axis=1)
+    shapes = (first_block.shape, second_block.shape, third_block.shape)
+    by_kernel = all(fits(*shape, members, split) for shape, split in zip(shapes, SPLITS))
+    if by_kernel:
+        first = gather_weight(first_block, members, shard_count, SPLITS[0], 3)
+    else:
+        first = lax.all_gather(first_block, "shard", axis=0, tiled=True)
+        second = lax.all_gather(second_block, "shard", axis=0, tiled=True)
+        third = lax.all_gather(third_block, "shard", axis=0, tiled=True)
+    full_qkv = first[:, : 3 * attn_width]
+    full_value = first[:, 3 * attn_width : 4 * attn_width]
+    full_point = first[:, 4 * attn_width : 5 * attn_width]
+    full_small = first[:, 5 * attn_width :]
+    full_span = full_small.reshape(shard_count, width_rows, 128)[:, :head_rows, : HEADS * KERNEL]
+    full_span = full_span.reshape(attn_width, HEADS * KERNEL)
+    full_depth = full_small[:, 64 : 64 + KERNEL].T
+    attn_gain_full, attn_bias_full, out_gain_full, out_bias_full = full_small[:, 64 + KERNEL : 68 + KERNEL].T
     rows_ext = with_halo(hidden_in, (("ctx", 1),), half_kernel)
     mixed_qkv = jnp.einsum("sti,io->sto", hidden_in, full_qkv, preferred_element_type=jnp.float32)
     query_low = mixed_qkv[..., :attn_width].astype(jnp.bfloat16)
     pair_low = mixed_qkv[..., attn_width:].astype(jnp.bfloat16)
-    members = lax.axis_size("ctx") // QUADS
     pair = pair_low.reshape(seq_count, local_rows, 2, HEADS, HEAD).transpose(0, 3, 1, 2, 4)
     pair = pair.reshape(QUADS, TRIPLE, local_rows, 2 * HEAD)
-    kv_all, q_all, out_all, lse, context_packed = attend_forward(pair, pack_heads(query_low), members)
+    kv_all, q_all, out_all, lse, context_packed, *gathered = attend_forward(
+        pair, pack_heads(query_low), members, shard_count,
+        (second_block, third_block) if by_kernel else (), SPLITS[1:] if by_kernel else (),
+    )
+    if by_kernel:
+        second, third = gathered
+    full_dense_attn = second[:, :model_width]
+    full_dense_conv = second[:, model_width : 2 * model_width]
+    full_inner = second[:, 2 * model_width :].reshape(D // GROUPS, GROUPS, -1).transpose(1, 0, 2)
+    full_outer = third.reshape(-1, GROUPS, D // GROUPS).transpose(1, 0, 2)
     context_low = unpack_heads(context_packed, seq_count)
     depth_fwd = full_depth.astype(jnp.float32)
     spread = rows_ext[:, 0:local_rows].astype(jnp.float32) * depth_fwd[0]
@@ -652,7 +1000,36 @@
     grad_conv_value = jnp.einsum(
         "sti,sta->ia", hidden_in, d_value_low, preferred_element_type=jnp.float32
     )
-    dq_packed, dkv = attend_backward(pack_heads(d_context_low), kv_all, q_all, out_all, lse, members)
+    def spread_rows(part, rows):
+        split = part.reshape(shard_count, rows, part.shape[1])
+        return jnp.pad(split, ((0, 0), (0, width_rows - rows), (0, 0))).reshape(model_width, -1)
+
+    middle = jnp.concatenate(
+        [
+            grad_conv_value,
+            grad_point,
+            spread_rows(grad_span, head_rows),
+            jnp.zeros((model_width, 64 - HEADS * KERNEL), jnp.float32),
+            grad_depth.T,
+            jnp.stack([grad_attn_gain, grad_attn_bias, grad_out_gain, grad_out_bias], axis=1),
+            jnp.zeros((model_width, 256 - 64 - KERNEL - 4), jnp.float32),
+        ],
+        axis=1,
+    )
+    second_part = jnp.concatenate([grad_dense_attn, grad_dense_conv, grad_ffn_inner[0], grad_ffn_inner[1]], axis=1)
+    third_part = jnp.concatenate([grad_ffn_outer[0], grad_ffn_outer[1]], axis=1)
+    parts = ()
+    part_splits = ()
+    if by_kernel:
+        whole_parts = (third_part, second_part, middle)
+        part_splits = (SPLITS[2], SPLITS[1], SPLITS[0])
+        parts = tuple(
+            (cut(one, members, shard_count, split), (one.shape[0] // shard_count, one.shape[1]))
+            for one, split in zip(whole_parts, part_splits)
+        )
+    dq_packed, dkv, *reduced = attend_backward(
+        pack_heads(d_context_low), kv_all, q_all, out_all, lse, members, shard_count, parts, part_splits
+    )
     d_query_attn = unpack_heads(dq_packed, seq_count).astype(jnp.float32)
     d_pair = dkv.reshape(seq_count, HEADS, local_rows, 2, HEAD).transpose(0, 2, 3, 1, 4)
     d_pair = d_pair.reshape(seq_count, local_rows, 2 * attn_width)
@@ -665,61 +1042,34 @@
         + jnp.einsum("sta,ia->sti", d_value_low, full_value, preferred_element_type=jnp.float32)
         + d_rows_conv
     )
-    shared = (
-        lax.psum_scatter(
-            grad_qkv.astype(jnp.bfloat16), "shard", scatter_dimension=0, tiled=True
-        ).astype(jnp.float32),
-        lax.psum_scatter(
-            grad_depth.astype(jnp.bfloat16), "shard", scatter_dimension=1, tiled=True
-        ).astype(jnp.float32),
-        lax.psum_scatter(
-            grad_point.astype(jnp.bfloat16), "shard", scatter_dimension=0, tiled=True
-        ).astype(jnp.float32),
-        lax.psum_scatter(
-            grad_span.astype(jnp.bfloat16), "shard", scatter_dimension=0, tiled=True
-        ).astype(jnp.float32),
-        lax.psum_scatter(
-            grad_conv_value.astype(jnp.bfloat16), "shard", scatter_dimension=0, tiled=True
-        ).astype(jnp.float32),
-        lax.psum_scatter(
-            grad_dense_attn.astype(jnp.bfloat16), "shard", scatter_dimension=0, tiled=True
-        ).astype(jnp.float32),
-        lax.psum_scatter(
-            grad_dense_conv.astype(jnp.bfloat16), "shard", scatter_dimension=0, tiled=True
-        ).astype(jnp.float32),
-        lax.psum_scatter(
-            grad_attn_gain.astype(jnp.bfloat16), "shard", scatter_dimension=0, tiled=True
-        ).astype(jnp.float32),
-        lax.psum_scatter(
-            grad_attn_bias.astype(jnp.bfloat16), "shard", scatter_dimension=0, tiled=True
-        ).astype(jnp.float32),
-        lax.psum_scatter(
-            grad_ffn_inner.astype(jnp.bfloat16), "shard", scatter_dimension=1, tiled=True
-        ).astype(jnp.float32),
-        lax.psum_scatter(
-            grad_ffn_outer.astype(jnp.bfloat16), "shard", scatter_dimension=1, tiled=True
-        ).astype(jnp.float32),
-        lax.psum_scatter(
-            grad_out_gain.astype(jnp.bfloat16), "shard", scatter_dimension=0, tiled=True
-        ).astype(jnp.float32),
-        lax.psum_scatter(
-            grad_out_bias.astype(jnp.bfloat16), "shard", scatter_dimension=0, tiled=True
-        ).astype(jnp.float32),
-    )
+    first_part = jnp.pad(grad_qkv, ((0, 0), (0, 128)))
+    if by_kernel:
+        third_sum, second_sum, middle_sum = reduced
+        first_sum = reduce_weight(first_part, members, shard_count, SPLITS[0], 4)
+    else:
+        first_sum, second_sum, third_sum, middle_sum = (
+            lax.psum(lax.psum_scatter(one.astype(BF), "shard", scatter_dimension=0, tiled=True), "ctx")
+            for one in (first_part, second_part, third_part, middle)
+        )
+    first_sum, second_sum, third_sum, middle_sum = (
+        one.astype(F32) for one in (first_sum, second_sum, third_sum, middle_sum)
+    )
+    edge = 2 * attn_width
+    norms = middle_sum[:, edge + 64 + KERNEL : edge + 68 + KERNEL].T
     summed = (
-        lax.psum(shared[0].astype(jnp.bfloat16), "ctx").astype(jnp.float32),
-        lax.psum(shared[1].astype(jnp.bfloat16), "ctx").astype(jnp.float32),
-        lax.psum(shared[2].astype(jnp.bfloat16), "ctx").astype(jnp.float32),
-        lax.psum(shared[3].astype(jnp.bfloat16), "ctx").astype(jnp.float32),
-        lax.psum(shared[4].astype(jnp.bfloat16), "ctx").astype(jnp.float32),
-        lax.psum(shared[5].astype(jnp.bfloat16), "ctx").astype(jnp.float32),
-        lax.psum(shared[6].astype(jnp.bfloat16), "ctx").astype(jnp.float32),
-        lax.psum(shared[7].astype(jnp.bfloat16), "ctx").astype(jnp.float32),
-        lax.psum(shared[8].astype(jnp.bfloat16), "ctx").astype(jnp.float32),
-        lax.psum(shared[9].astype(jnp.bfloat16), "ctx").astype(jnp.float32),
-        lax.psum(shared[10].astype(jnp.bfloat16), "ctx").astype(jnp.float32),
-        lax.psum(shared[11].astype(jnp.bfloat16), "ctx").astype(jnp.float32),
-        lax.psum(shared[12].astype(jnp.bfloat16), "ctx").astype(jnp.float32),
+        first_sum[:, : 3 * attn_width],
+        middle_sum[:, edge + 64 : edge + 64 + KERNEL].T,
+        middle_sum[:, attn_width:edge],
+        middle_sum[:head_rows, edge : edge + HEADS * KERNEL],
+        middle_sum[:, :attn_width],
+        second_sum[:, :model_width],
+        second_sum[:, model_width : 2 * model_width],
+        norms[0],
+        norms[1],
+        second_sum[:, 2 * model_width :].reshape(head_rows, GROUPS, -1).transpose(1, 0, 2),
+        third_sum.reshape(-1, GROUPS, D // GROUPS).transpose(1, 0, 2),
+        norms[2],
+        norms[3],
     )
     result_grads = tuple(summed)
     return (layer_out, grad_in) + result_grads

time: 912 us -> 628 us (0.69)
  waiting for transfers between devices: 236 us -> 0.01 us
  blocking collectives: 168 us -> 0 us
  Pallas kernels: 162 us -> 249 us
  local copies, waits for them, and re-layouts: 112 us -> 160 us
  between operations: 17.3 us -> 2.83 us
  matrix products: 135 us -> 123 us
    reduce_scatter x5 -> x0, waiting for transfers between devices: 166 us -> none  [the longest x1 49.8 us: shards(): lax.psum_scatter(grad_ffn_inner.astype(jnp.bfloat16), 'shard', scatter_di...]
    all_gather x6 -> x0, blocking collectives: 115 us -> none  [the longest x1 23.4 us: shards(): lax.all_gather(dense_attn, 'shard', axis=0, tiled=True)]
    pallas_call x2 -> x4, Pallas kernels: 162 us -> 249 us  [the longest x1 113 us: attend_backward(): pl.pallas_call(functools.partial(attend_backward_kernel, members, shards,...]
    psum x1 -> x0, waiting for transfers between devices: 42 us -> none  [shards(): lax.psum(shared[0].astype(jnp.bfloat16), 'ctx').astype(jnp.float32)]
    unnamed x2 -> x0, blocking collectives: 30.8 us -> none
    unnamed x17 -> x0, waiting for transfers between devices: 25.1 us -> none
    psum x1 -> x0, blocking collectives: 22.8 us -> none  [shards(): lax.psum(shared[1].astype(jnp.bfloat16), 'ctx').astype(jnp.float32)]
    reshape x0 -> x8, local copies, waits for them, and re-layouts: none -> 14.4 us  [the longest x2 5.34 us: cut(): part.astype(BF)]
  transfers between devices with their start and end apart: 17 -> 4, of which waited for: 9 -> 0; matrix products, arithmetic and copies ran while one was open for 19% -> 12% of each run, Pallas kernels for 7% -> 17%
where the time goes in v2:
time: 628 us; the launch traced here: 618 us
  Pallas kernels  249 us (40%)
  local copies, waits for them, and re-layouts  160 us (25%)
  matrix products  123 us (20%)
  other arithmetic  75.3 us (12%)
  starting transfers between devices  7.69 us (1%)
    pallas_call x1, Pallas kernels, attend_backward(): pl.pallas_call(functools.partial(attend_backward_kernel, members, shards,...  113 us
    pallas_call x1, Pallas kernels, attend_forward(): pl.pallas_call(functools.partial(attend_forward_kernel, members, shards,...  76.2 us
    dot_general x1, matrix products, shards(): jnp.einsum('stgi,gio->stgo', hidden_low, full_inner, preferred_element_ty...  32.6 us
    pallas_call x1, Pallas kernels, gather_weight(): pl.pallas_call(functools.partial(gather_kernel, members, shards, split),...  31.1 us
    pallas_call x1, Pallas kernels, reduce_weight(): pl.pallas_call(functools.partial(reduce_kernel, members, shards, split),...  29.3 us
    unnamed x231, local copies, waits for them, and re-layouts  17.3 us
    dot_general x1, matrix products, shards(): jnp.einsum('stgi,goi->stgo', d_outer_low, full_outer, preferred_element_t...  13.5 us
    convert_element_type x4, local copies, waits for them, and re-layouts, cut(): part.astype(BF)  12.6 us
  transfers between devices with their start and end apart: 4, of which 0 were waited for; matrix products, arithmetic and copies ran while one was open for 12% of the time, Pallas kernels for 17%

profile of v2, /device:TPU:0, one launch (start us, length us, event | category | flops | bytes accessed | tf_op | source)
XLA Modules:
  0.0 617.5 jit_solution(18085025354831135874)
XLA Ops:
  2.1 2.9 collective-permute-start
  10.8 31.1 %shard_map.262 = bf16[768,2048]{1,0:T(8,128)(2,1)} custom-call(bf16[192,2048]{1,0:T(8,128)(2,1)} %concatenate.59.shard_ref), custom_call_target="tpu_custom_call" | custom-call | tf_op jit(solution)/shard_map/pallas_call | solution.py:366
  44.0 3.5 fusion.30
  53.2 3.0 reshape.219
  62.0 2.7 copy.280.refs_0_
  66.5 76.2 %shard_map.263 = (bf16[3,4,2,512,128]{4,3,2,1,0:T(8,128)(2,1)}, bf16[3,4,256,128]{3,2,1,0:T(8,128)(2,1)}, f32[3,4,256,128]{3,2,1,0:T(8,128)}, f32[3,4,2,2,8,128]...) custom-call(bf16[4,3,512,128]{3,2,1,0:T(8,128)(2,1)} %copy.280.refs_0_, ...), custom_call_target="tpu_custom_call" | custom-call | flops 6442450944 | bytes 8388608 | tf_op jit(solution)/shard_map/pallas_call | solution.py:542
  146.3 4.2 fusion.107
  154.2 4.3 copy.454
  158.5 4.3 copy.389
  163.7 7.4 %fusion.39 = bf16[2,512,768]{2,1,0:T(8,128)(2,1)S(1)} fusion(bf16[2,512,768]{2,1,0:T(8,128)(2,1)} %param.15, bf16[2,4,768]{2,1,0:T(4,128)(2,1)} %collective-permute-done, f32[768]{0:T(1024)S(1)} %copy-done.89, f32[768]{0:T(1024)S(1)} %copy-done.91, f32[768]{0:T(1024)S(1)} %copy-done.93, f32[768]{0:T(1024)S(1)} %copy-done.95, f32[768]{0:T(1024)S(1)} %copy-done.97, ...), kind=kLoop, calls=%fused_computation.84 | loop fusion | flops 30670848 | bytes 9477120 | tf_op jit(solution)/shard_map/convert_element_type | solution.py:866
  178.5 3.6 add_convert_fusion.2
  182.2 2.6 fusion.144
  188.2 4.4 reshape.228
  192.5 4.9 copy.323
  197.4 32.6 %fusion.11 = (bf16[2,512,2,1536]{1,3,0,2:T(8,128)(2,1)S(1)}, f32[2,512,2,1536]{1,3,0,2:T(8,128)}, f32[2,1536,2,512]{3,1,2,0:T(8,128)}) fusion(bf16[2,384,1536,1]{1,2,3,0:T(8,128)(2,1)} %bitcast.375, bf16[2,512,2,384]{1,3,0,2:T(8,128)(2,1)} %copy.323), kind=kOutput, calls=%fused_computation.19 | convolution fusion | flops 2620391424 | bytes 35389440 | tf_op jit(solution)/shard_map/stgi,gio->stgo/dot_general | solution.py:893
  230.1 2.7 copy-done.108
  232.8 4.4 fusion.59
  237.1 5.8 copy.313
  243.0 5.7 reshape.229
  248.7 3.7 fusion.134
  256.4 4.7 bitcast_convert_fusion.1
  261.1 13.5 %fusion.8 = bf16[2,512,2,1536]{1,3,0,2:T(8,128)(2,1)} fusion(f32[2,512,2,1536]{1,3,0,2:T(8,128)} %get-tuple-element.150, f32[2,1536,2,512]{3,1,2,0:T(8,128)} %get-tuple-element.203, bf16[192,2,8,384]{3,2,1,0:T(8,128)(2,1)S(1)} %bitcast.374, bf16[2,64,2,8,384]{4,3,2,1,0:T(8,128)(2,1)S(1)} %bitcast.380), kind=kOutput, calls=%fused_computation.11 | convolution fusion | flops 2459959296 | bytes 35389440 | tf_op jit(solution)/shard_map/stgi,goi->stgo/dot_general | solution.py:913
  274.6 8.3 %bitcast_convert_fusion = bf16[2,384,1536]{2,1,0:T(8,128)(2,1)} fusion(bf16[2,512,2,384]{1,3,0,2:T(8,128)(2,1)S(1)} %copy-done.43, bf16[2,512,2,1536]{1,3,0,2:T(8,128)(2,1)} %fusion.8), kind=kOutput, calls=%fused_computation.45 | convolution fusion | flops 2417098752 | bytes 10223616 | tf_op jit(solution)/shard_map/stgi,stgo->gio/dot_general | solution.py:917
  282.9 4.3 convolution_bitcast_fusion.1
  287.2 5.8 copy.317
  293.0 5.9 reshape.231
  298.9 6.8 %multiply_reduce_fusion = (bf16[768]{0:T(1024)(128)(2,1)}, f32[2,512]{1,0:T(2,128)S(1)}, f32[2,512]{1,0:T(2,128)S(1)}, bf16[768]{0:T(1024)(128)(2,1)}, f32[2,512...) fusion(f32[2,512,768]{2,1,0:T(8,128)} %copy-done, f32[2,512]{1,0:T(2,128)S(1)} %add_rsqrt_fusion.1, ...), kind=kLoop, calls=%fused_computation.99 | loop fusion | flops 16511488 | bytes 15773696 | tf_op jit(solution)/shard_map/reduce_sum | solution.py:43
  310.7 3.0 convolution_convert_fusion.1
  315.7 7.7 %multiply_reduce_fusion.5 = (f32[2,512,6]{1,2,0:T(8,128)S(1)}, f32[2,512,6]{1,2,0:T(8,128)S(1)}, f32[2,512,6]{1,2,0:T(8,128)S(1)}, f32[2,512,6]{1,2,0:T(8,128)S(...) fusion(f32[2,512,6,64]{1,3,2,0:T(8,128)S(1)} %bitcast.361, ...), kind=kLoop, calls=%fused_computation.148 | loop fusion | flops 10561536 | bytes 30326784 | tf_op jit(solution)/shard_map/reduce_sum | solution.py:942
  329.8 9.2 %pad_add_fusion.1 = f32[2,520,6,64]{1,3,2,0:T(8,128)} fusion(f32[2,512,6,64]{1,3,2,0:T(8,128)} %get-tuple-element.177, f32[2,512,6,64]{1,3,2,0:T(8,128)} %get-tuple-element.176, f32[2,512,6,64]{1,3,2,0:T(8,128)} %get-tuple-element.175, f32[2,512,6,64]{1,3,2,0:T(8,128)} %get-tuple-element.174, f32[2,512,6,64]{1,3,2,0:T(8,128)} %get-tuple-element.173, ...), kind=kLoop, calls=%fused_computation.123 | loop fusion | flops 3194880 | bytes 15753216 | tf_op jit(solution)/shard_map/add | solution.py:976
  339.0 2.9 copy.348
  342.0 10.2 %fusion.47 = (bf16[768]{0:T(1024)(128)(2,1)}, bf16[768]{0:T(1024)(128)(2,1)}, bf16[768]{0:T(1024)(128)(2,1)}, bf16[768]{0:T(1024)(128)(2,1)S(1)}, bf16[768]{0:T(...) fusion(bf16[2,516,768]{2,1,0:T(8,128)(2,1)S(1)} %copy-done.5, ...), kind=kOutput, calls=%fused_computation.92 | convolution fusion | flops 639755520 | bytes 29729280 | tf_op jit(solution)/shard_map/sta,ia->sti/dot_general | solution.py:958
  352.2 3.0 broadcast_multiply_fusion.8
  355.2 5.4 pad_add_fusion
  374.5 5.7 convert_element_type.251
  387.2 2.9 reshape.232
  397.8 2.8 pad_maximum_fusion.1
  405.0 7.6 %concatenate.73 = bf16[768,1024]{0,1:T(8,128)(2,1)S(1)} concatenate(bf16[768,384]{0,1:T(8,128)(2,1)} %fusion.86, bf16[768,384]{0,1:T(8,128)(2,1)} %fusion.85, bf16[768,54]{0,1:T(8,128)(2,1)S(1)} %reshape.237, bf16[768,10]{0,1:T(8,128)(2,1)} %broadcast_in_dim.63, bf16[768,9]{0,1:T(8,128)(2,1)S(1)} %bitcast.398, bf16[768,1]{0,1:T(2,128)(2,1)} %stack.82, bf16[768,1]{0,1:T(2,128)(2,1)} %stack.83, ...), dimensions={1} | concatenate | bytes 3145728 | tf_op jit(solution)/shard_map/concatenate | solution.py:1007
  414.3 2.9 convert_element_type.256
  418.6 112.6 %shard_map.264 = (bf16[4,3,256,128]{3,2,1,0:T(8,128)(2,1)}, bf16[4,3,512,128]{3,2,1,0:T(8,128)(2,1)}, bf16[384,768]{1,0:T(8,128)(2,1)}, bf16[96,4608]{1,0:T(8,128)(2,1)}, bf16[192,1024]{1,0:T(8,128)(2,1)}) custom-call(bf16[4,3,256,128]{3,2,1,0:T(8,128)(2,1)} %copy.354.refs_0_, bf16[3,4,2,512,128]{4,3,2,1,0:T(8,128)(2,1)} %get-tuple-element.30.refs_1_, ...), custom_call_target="tpu_custom_call" | custom-call | flops 16106127360 | bytes 8388608 | tf_op jit(solution)/shard_map/pallas_call | solution.py:740
  538.0 3.9 copy.356
  541.9 3.6 reshape.247
  545.4 3.2 add_convert_fusion.1
  555.7 4.7 fusion.53
  560.3 3.9 fusion.62
  575.8 3.3 copy.456
  579.1 29.3 %shard_map.265 = bf16[192,1280]{1,0:T(8,128)(2,1)} custom-call(bf16[2,4,4,48,640]{4,3,2,1,0:T(8,128)(2,1)} %bitcast.353), custom_call_target="tpu_custom_call" | custom-call | tf_op jit(solution)/shard_map/pallas_call | solution.py:391
  610.4 6.7 %slice_add_fusion = f32[2,512,768]{2,1,0:T(8,128)} fusion(f32[2,512,1152]{2,1,0:T(8,128)} %copy-done.19, f32[2,512,768]{2,1,0:T(8,128)} %fusion.62, bf16[768,2048]{1,0:T(8,128)(2,1)} %shard_map.262, f32[2,512]{1,0:T(2,128)S(1)} %broadcast_multiply_fusion.18, f32[2,512,768]{2,1,0:T(8,128)S(1)} %copy-done.2, f32[2,512]{1,0:T(2,128)S(1)} %broadcast_multiply_fusion.23, ...), kind=kOutput, calls=%fused_computation.98 | convolution fusion | flops 612237312 | bytes 17910784 | tf_op jit(solution)/shard_map/sta,ia->sti/dot_general | solution.py:1042
  (375 shorter events, 120.9 us)
Async XLA Ops:
  0.6 7.2 %copy-start.99 = (bf16[96,54]{0,1:T(8,128)(2,1)S(1)}, bf16[96,54]{0,1:T(8,128)(2,1)}, u32[]{:S(2)}) copy-start(bf16[96,54]{0,1:T(8,128)(2,1)} %param.20) | copy-start | bytes 31108
  0.7 7.3 %copy-start.103 = (bf16[9,192]{1,0:T(8,128)(2,1)S(1)}, bf16[9,192]{1,0:T(8,128)(2,1)}, u32[]{:S(2)}) copy-start(bf16[9,192]{1,0:T(8,128)(2,1)} %param.18) | copy-start | bytes 10372
  0.7 7.4 %copy-start.104 = (bf16[192]{0:T(256)(128)(2,1)S(1)}, bf16[192]{0:T(256)(128)(2,1)}, u32[]{:S(2)}) copy-start(bf16[192]{0:T(256)(128)(2,1)} %param.24) | copy-start | bytes 1156
  0.7 7.5 %copy-start.105 = (bf16[192]{0:T(256)(128)(2,1)S(1)}, bf16[192]{0:T(256)(128)(2,1)}, u32[]{:S(2)}) copy-start(bf16[192]{0:T(256)(128)(2,1)} %param.25) | copy-start | bytes 1156
  0.7 7.6 %copy-start.106 = (bf16[192]{0:T(256)(128)(2,1)S(1)}, bf16[192]{0:T(256)(128)(2,1)}, u32[]{:S(2)}) copy-start(bf16[192]{0:T(256)(128)(2,1)} %param.28) | copy-start | bytes 1156
  0.7 7.7 %copy-start.107 = (bf16[192]{0:T(256)(128)(2,1)S(1)}, bf16[192]{0:T(256)(128)(2,1)}, u32[]{:S(2)}) copy-start(bf16[192]{0:T(256)(128)(2,1)} %param.29) | copy-start | bytes 1156
  2.1 161.5 %collective-permute-start = (bf16[2,4,768]{2,1,0:T(4,128)(2,1)}, bf16[2,4,768]{2,1,0:T(4,128)(2,1)}, u32[]{:S(2)}, u32[]{:S(2)}) collective-permute-start(bf16[2,4,768]{2,1,0:T(4,128)(2,1)} %get-tuple-element.178), channel_id=1, source_target_pairs={{0,4},{4,8},{8,12},{12,16},{16,20},{20,24},{24,28},{1,5},{5,9},{9,... | collective-permute-start | bytes 36872 | tf_op jit(solution)/shard_map/ppermute | solution.py:27
  5.0 157.8 %collective-permute-start.1 = (bf16[2,4,768]{2,1,0:T(4,128)(2,1)}, bf16[2,4,768]{2,1,0:T(4,128)(2,1)}, u32[]{:S(2)}, u32[]{:S(2)}) collective-permute-start(bf16[2,4,768]{2,1,0:T(4,128)(2,1)} %get-tuple-element.179), channel_id=1, source_target_pairs={{4,0},{8,4},{12,8},{16,12},{20,16},{24,20},{28,24},{5,1},{9,5},{13... | collective-permute-start | bytes 36872 | tf_op jit(solution)/shard_map/ppermute | solution.py:30
  8.6 35.4 %copy-start.10 = (bf16[2,512,768]{2,1,0:T(8,128)(2,1)S(1)}, bf16[2,512,768]{2,1,0:T(8,128)(2,1)}, u32[]{:S(2)}) copy-start(bf16[2,512,768]{2,1,0:T(8,128)(2,1)} %param.15) | copy-start | bytes 4718596
  53.2 110.4 %copy-start.79 = (f32[768]{0:T(1024)}, f32[768]{0:T(1024)S(1)}, u32[]{:S(2)}) copy-start(f32[768]{0:T(1024)S(1)} %get-tuple-element.129) | copy-start | bytes 9220
  53.2 110.5 %copy-start.81 = (f32[768]{0:T(1024)}, f32[768]{0:T(1024)S(1)}, u32[]{:S(2)}) copy-start(f32[768]{0:T(1024)S(1)} %get-tuple-element.135) | copy-start | bytes 9220
  53.2 7.5 %slice-start.1 = ((bf16[2,512,1152]{1,2,0:T(8,128)(2,1)}), bf16[2,512,768]{1,2,0:T(8,128)(2,1)S(1)}, s32[]{:S(2)}) async-start(bf16[2,512,1152]{1,2,0:T(8,128)(2,1)} %copy-done.22), calls=%async_computation.1 | async-start | bytes 3145728 | tf_op jit(solution)/shard_map/slice | solution.py:845
  145.4 6.1 copy-start.28
  154.0 8.8 %copy-start.48 = (bf16[4,96,54]{2,1,0:T(8,128)(2,1)}, bf16[4,96,54]{2,1,0:T(8,128)(2,1)S(1)}, u32[]{:S(2)}) copy-start(bf16[4,96,54]{2,1,0:T(8,128)(2,1)S(1)} %slice.401) | copy-start | bytes 124420
  158.5 5.1 copy-start.83
  158.5 5.1 copy-start.85
  158.5 5.2 copy-start.89
  158.5 5.2 copy-start.91
  158.5 5.2 copy-start.93
  158.5 5.2 copy-start.95
  158.5 5.2 copy-start.97
  163.6 7.6 %copy-start.4 = (bf16[2,516,768]{2,1,0:T(8,128)(2,1)}, bf16[2,516,768]{2,1,0:T(8,128)(2,1)S(1)}, u32[]{:S(2)}) copy-start(bf16[2,516,768]{2,1,0:T(8,128)(2,1)S(1)} %constant_dynamic-update-slice_fusion) | copy-start | bytes 4755460
  163.7 7.5 %copy-start.20 = (bf16[768,2048]{1,0:T(8,128)(2,1)S(1)}, bf16[768,2048]{1,0:T(8,128)(2,1)}, u32[]{:S(2)}) copy-start(bf16[768,2048]{1,0:T(8,128)(2,1)} %shard_map.262) | copy-start | bytes 9437188
  163.7 7.5 %copy-start.23 = (bf16[2,512,1152]{1,2,0:T(8,128)(2,1)S(1)}, bf16[2,512,1152]{1,2,0:T(8,128)(2,1)}, u32[]{:S(2)}) copy-start(bf16[2,512,1152]{1,2,0:T(8,128)(2,1)} %copy-done.22) | copy-start | bytes 7077892
  197.4 35.3 %copy-start.41 = (bf16[1536,768]{0,1:T(8,128)(2,1)S(1)}, bf16[1536,768]{0,1:T(8,128)(2,1)}, u32[]{:S(2)}) copy-start(bf16[1536,768]{0,1:T(8,128)(2,1)} %copy.454) | copy-start | bytes 7077892
  261.1 13.5 %copy-start.43 = (bf16[2,512,2,384]{1,3,0,2:T(8,128)(2,1)S(1)}, bf16[2,512,2,384]{1,3,0,2:T(8,128)(2,1)}, u32[]{:S(2)}) copy-start(bf16[2,512,2,384]{1,3,0,2:T(8,128)(2,1)} %copy.323) | copy-start | bytes 4718596
  274.6 8.4 %copy-start.40 = (bf16[384,3072]{0,1:T(8,128)(2,1)S(1)}, bf16[384,3072]{0,1:T(8,128)(2,1)}, u32[]{:S(2)}) copy-start(bf16[384,3072]{0,1:T(8,128)(2,1)} %copy.389) | copy-start | bytes 7077892
  274.6 8.4 %copy-start.109 = (bf16[2,512,2,1536]{1,3,0,2:T(8,128)(2,1)S(1)}, bf16[2,512,2,1536]{1,3,0,2:T(8,128)(2,1)}, u32[]{:S(2)}) copy-start(bf16[2,512,2,1536]{1,3,0,2:T(8,128)(2,1)} %fusion.8) | copy-start | bytes 18874372
  298.9 6.8 %copy-start.1 = (f32[2,512,768]{2,1,0:T(8,128)S(1)}, f32[2,512,768]{2,1,0:T(8,128)}, u32[]{:S(2)}) copy-start(f32[2,512,768]{2,1,0:T(8,128)} %copy-done) | copy-start | bytes 9437188
  310.7 5.0 copy-start.60
  310.7 5.0 copy-start.62
  310.7 5.0 copy-start.64
  310.7 5.0 copy-start.66
  310.7 5.0 copy-start.68
  310.7 5.0 copy-start.70
  310.7 5.0 copy-start.72
  341.9 10.2 %copy-start.80 = (f32[768]{0:T(1024)S(1)}, f32[768]{0:T(1024)}, u32[]{:S(2)}) copy-start(f32[768]{0:T(1024)} %copy-done.79) | copy-start | bytes 9220
  342.0 10.2 %copy-start.82 = (f32[768]{0:T(1024)S(1)}, f32[768]{0:T(1024)}, u32[]{:S(2)}) copy-start(f32[768]{0:T(1024)} %copy-done.81) | copy-start | bytes 9220
  342.0 10.2 %copy-start.84 = (f32[768]{0:T(1024)S(1)}, f32[768]{0:T(1024)}, u32[]{:S(2)}) copy-start(f32[768]{0:T(1024)} %get-tuple-element.136) | copy-start | bytes 9220
  342.0 10.2 %copy-start.86 = (f32[768]{0:T(1024)S(1)}, f32[768]{0:T(1024)}, u32[]{:S(2)}) copy-start(f32[768]{0:T(1024)} %get-tuple-element.137) | copy-start | bytes 9220
  355.2 5.4 copy-start.8
  365.3 31.6 %collective-permute-start.2 = (bf16[2,4,1152]{2,1,0:T(4,128)(2,1)S(1)}, bf16[2,4,1152]{2,1,0:T(4,128)(2,1)S(1)}, u32[]{:S(2)}, u32[]{:S(2)}) collective-permute-start(bf16[2,4,1152]{2,1,0:T(4,128)(2,1)S(1)} %get-tuple-element.163), channel_id=1, source_target_pairs={{0,4},{4,8},{8,12},{12,16},{16,20},{20,24},{24,28},{1,5},{5,9},{9,... | collective-permute-start | bytes 55304 | tf_op jit(solution)/shard_map/ppermute | solution.py:27
  367.5 29.4 %collective-permute-start.3 = (bf16[2,4,1152]{2,1,0:T(4,128)(2,1)S(1)}, bf16[2,4,1152]{2,1,0:T(4,128)(2,1)}, u32[]{:S(2)}, u32[]{:S(2)}) collective-permute-start(bf16[2,4,1152]{2,1,0:T(4,128)(2,1)S(1)} %get-tuple-element.164), channel_id=1, source_target_pairs={{4,0},{8,4},{12,8},{16,12},{20,16},{24,20},{28,24},{5,1},{9,5},{13... | collective-permute-start | bytes 55304 | tf_op jit(solution)/shard_map/ppermute | solution.py:30
  531.3 5.3 copy-start.50
  538.0 7.5 %copy-start.15 = (f32[2,512,384]{1,2,0:T(8,128)S(1)}, f32[2,512,384]{1,2,0:T(8,128)}, u32[]{:S(2)}) copy-start(f32[2,512,384]{1,2,0:T(8,128)} %copy-done.14) | copy-start | bytes 4718596
  575.8 34.6 %copy-start.2 = (f32[2,512,768]{2,1,0:T(8,128)S(1)}, f32[2,512,768]{2,1,0:T(8,128)}, u32[]{:S(2)}) copy-start(f32[2,512,768]{2,1,0:T(8,128)} %copy-done) | copy-start | bytes 9437188
  575.8 34.6 %copy-start.7 = (f32[2,512,768]{2,1,0:T(8,128)S(1)}, f32[2,512,768]{2,1,0:T(8,128)}, u32[]{:S(2)}) copy-start(f32[2,512,768]{2,1,0:T(8,128)} %copy-done.6) | copy-start | bytes 9437188
  575.8 34.6 %copy-start.78 = (f32[2,512]{1,0:T(2,128)S(1)}, f32[2,512]{1,0:T(2,128)}, u32[]{:S(2)}) copy-start(f32[2,512]{1,0:T(2,128)} %copy-done.77) | copy-start | bytes 12292
  (70 other events, 211.3 us)
